TPU v7x, 32 devices: a whole 2x2x4 slice. The times are simulated.
32 devices in a mesh: group: 4 (over z), tok: 8 (over y, x, core).
Axes of the slice: x: 2, y: 2, z: 4, core: 2. Of those that a mesh axis runs over, the one named last changes fastest.
Arguments:
- tokens: bfloat16 [2048, 1792], P(('group', 'tok')), may hold values from -6 to 6
- norm_gains: float32 [2, 1792], replicated, may hold values from 0.25 to 1.75
- qk_weight: bfloat16 [2, 256, 1792], replicated, may hold values from -0.125 to 0.125
- mixer_weight: bfloat16 [3, 1792, 1792], P(None, 'tok'), may hold values from -0.125 to 0.125
- conv_weight: float32 [3, 1792], P(None, 'tok'), may hold values from -1 to 1
- out_weight: bfloat16 [2, 1792, 1792], P(None, 'tok'), may hold values from -0.09375 to 0.09375
- ffn_weight: bfloat16 [2, 4864, 1792], P(None, 'tok'), may hold values from -0.125 to 0.125
- down_weight: bfloat16 [4864, 1792], P('tok'), may hold values from -0.078125 to 0.078125
- cached_states: float32 [32, 273, 1792], P('group', None, 'tok'), may hold values from -8 to 8
- cached_norms: float32 [32, 273, 16], P('group'), as said below
- conv_cache: bfloat16 [32, 2, 1792], P('group', None, 'tok'), may hold values from -6 to 6
- cached_lengths: int32 [32], P('group'), may hold values from 0 to 31744
- new_lengths: int32 [4, 8], P('group'), may hold values from 1 to 504, as said below
- state_source: int32 [32, 1], replicated, may hold values from 0 to 3; in each aligned block of 8 rows (0 to 7, 8 to 15, ...) at most 2 rows name the same one
Outputs:
- layer_out: bfloat16 [2048, 1792], P(('group', 'tok'))
- new_states: float32 [32, 273, 1792], P('group', None, 'tok')
- new_norms: float32 [32, 273, 16], P('group')
- new_cache: bfloat16 [32, 2, 1792], P('group', None, 'tok')
Inputs may be any that keep to these rules, and one draw needn't show every extreme that they name: `new_lengths`: the 8 lengths of a group sum to 512; in every group at least two requests have one new token and one has exactly 504. `state_source`: among the 8 requests of one group, at most 2 name the same group. For every vector x of 16 entries and every slot and head, phi(x) . cached_norms[slot][:, head] is positive.
All inputs are finite; a program needn't handle non-finite values.
Results may differ from a plain program's by a relative error of at most 0.02.
Values may be sent and summed in bfloat16 or wider, within the bound.
A program may use at most 128 MiB of HBM per device.

v0:
```python
import math

import jax
import jax.numpy as jnp
from jax import lax
from jax.sharding import PartitionSpec as P

epsilon = 1e-05
quad_scale = 0.25 / math.sqrt(2.0)
highest = lax.Precision.HIGHEST


def rms_scale(inputs, gain_row):
    widened = inputs.astype(jnp.float32)
    mean_sq = jnp.mean(widened * widened, axis=-1, keepdims=True)
    return widened * lax.rsqrt(mean_sq + epsilon) * gain_row


def taylor_features(vectors):
    row_count = vectors.shape[0]
    feat_count = vectors.shape[1]
    outer_terms = (vectors[:, :, None] * vectors[:, None, :]).reshape(
        row_count, feat_count * feat_count
    )
    return jnp.concatenate(
        [jnp.ones((row_count, 1), jnp.float32), 0.5 * vectors, quad_scale * outer_terms], axis=1
    )


def segment_layout(lengths, all_rows):
    request_ends = jnp.cumsum(lengths)
    request_starts = request_ends - lengths
    position = jnp.arange(all_rows, dtype=jnp.int32)
    segment = jnp.sum((position[:, None] >= request_ends[None, :]).astype(jnp.int32), axis=1)
    member = segment[:, None] == jnp.arange(lengths.shape[0], dtype=jnp.int32)[None, :]
    offset = position - jnp.sum(jnp.where(member, request_starts[None, :], 0), axis=1)
    return (request_ends, segment, member, offset)


def head_attention(
    queries, keys_head, values_head, state_head, norm_head, segment, member, query_block
):
    all_rows = queries.shape[0]
    requests, phi_size, value_width = state_head.shape
    state_flat = jnp.transpose(state_head, (1, 0, 2)).reshape(phi_size, requests * value_width)
    position = jnp.arange(all_rows, dtype=jnp.int32)
    pieces_out = []
    for first_row in range(0, all_rows, query_block):
        query_rows = queries[first_row : first_row + query_block]
        scores = lax.dot_general(query_rows, keys_head, (((1,), (1,)), ((), ())), precision=highest)
        kernel = 1.0 + 0.25 * scores + scores * scores / 32.0
        allowed = (segment[first_row : first_row + query_block, None] == segment[None, :]) & (
            position[None, :] <= position[first_row : first_row + query_block, None]
        )
        kernel = jnp.where(allowed, kernel, 0.0)
        local_den = jnp.sum(kernel, axis=1)
        local_num = jnp.dot(
            kernel.astype(jnp.bfloat16), values_head, preferred_element_type=jnp.float32
        )
        features = taylor_features(query_rows)
        carried = jnp.dot(features, state_flat, precision=highest).reshape(
            query_block, requests, value_width
        )
        owner = member[first_row : first_row + query_block]
        carried_num = jnp.sum(jnp.where(owner[:, :, None], carried, 0.0), axis=1)
        carried_den = jnp.sum(
            jnp.where(owner, jnp.dot(features, norm_head.T, precision=highest), 0.0), axis=1
        )
        pieces_out.append((local_num + carried_num) / (local_den + carried_den)[:, None])
    return jnp.concatenate(pieces_out, axis=0).astype(jnp.bfloat16)


def state_update(keys_head, values_head, member, state_head, norm_head):
    all_rows = keys_head.shape[0]
    requests, phi_size, value_width = state_head.shape
    features = taylor_features(keys_head)
    weights = member.astype(jnp.float32)
    spread = (weights[:, :, None] * values_head.astype(jnp.float32)[:, None, :]).reshape(
        all_rows, requests * value_width
    )
    added_state = lax.dot_general(features, spread, (((0,), (0,)), ((), ())), precision=highest)
    added_state = jnp.transpose(added_state.reshape(phi_size, requests, value_width), (1, 0, 2))
    norm_added = lax.dot_general(weights, features, (((0,), (0,)), ((), ())), precision=highest)
    return (state_head + added_state, norm_head + norm_added)


def short_conv(
    inputs, conv_gate, conv_taps, conv_state, cached_length, lengths, request_ends, member, offset
):
    all_rows = inputs.shape[0]
    channels = inputs.shape[1]
    cached = conv_state.astype(jnp.float32)
    last_cached = cached[:, 1] * (cached_length >= 1).astype(jnp.float32)[:, None]
    second_cached = cached[:, 0] * (cached_length >= 2).astype(jnp.float32)[:, None]
    last_rows = jnp.sum(jnp.where(member[:, :, None], last_cached[None], 0.0), axis=1)
    second_rows = jnp.sum(jnp.where(member[:, :, None], second_cached[None], 0.0), axis=1)
    shift_one = jnp.concatenate([jnp.zeros((1, channels), jnp.float32), inputs[:-1]], axis=0)
    shift_two = jnp.concatenate([jnp.zeros((2, channels), jnp.float32), inputs[:-2]], axis=0)
    within = offset[:, None]
    prev_one = jnp.where(within >= 1, shift_one, last_rows)
    prev_two = jnp.where(within >= 2, shift_two, jnp.where(within == 1, last_rows, second_rows))
    convolved = conv_taps[0] * inputs + conv_taps[1] * prev_one + conv_taps[2] * prev_two
    conv_out = (convolved * conv_gate).astype(jnp.bfloat16)
    position = jnp.arange(all_rows, dtype=jnp.int32)
    at_end = position[None, :] == (request_ends - 1)[:, None]
    before_end = position[None, :] == (request_ends - 2)[:, None]
    final_rows = jnp.sum(jnp.where(at_end[:, :, None], inputs[None], 0.0), axis=1)
    penultimate = jnp.sum(jnp.where(before_end[:, :, None], inputs[None], 0.0), axis=1)
    penultimate = jnp.where((lengths >= 2)[:, None], penultimate, last_cached)
    return (conv_out, jnp.stack([penultimate, final_rows], axis=1).astype(jnp.bfloat16))


def down_term(hidden, down_weight):
    return jnp.dot(hidden, down_weight, preferred_element_type=jnp.float32)


def on_device(
    tokens,
    norm_gains,
    qk_weight,
    mixer_weight,
    conv_weight,
    out_weight,
    ffn_weight,
    down_weight,
    cached_states,
    cached_norms,
    conv_cache,
    cached_lengths,
    new_lengths,
    state_source,
):
    tok_rows = tokens.shape[0]
    model_width = tokens.shape[1]
    shards = lax.axis_size("tok")
    requests = cached_states.shape[0]
    phi_size = cached_states.shape[1]
    columns = cached_states.shape[2]
    head_count = cached_norms.shape[2]
    head_width = model_width // head_count
    feature = qk_weight.shape[1] // head_count
    heads_here = max(1, columns // head_width)
    head_cols = columns // heads_here
    all_rows = tok_rows * shards
    query_block = math.gcd(all_rows, 512)
    group_now = lax.axis_index("group")
    tok_now = lax.axis_index("tok")
    first_head = tok_now * columns // head_width
    sources = state_source[:, 0]
    own_sources = lax.dynamic_slice_in_dim(sources, group_now * requests, requests)
    conv_wide = conv_cache.astype(jnp.float32)
    wanted = own_sources * requests + jnp.arange(requests, dtype=jnp.int32)
    blanks = (
        jnp.zeros_like(cached_states),
        jnp.zeros_like(cached_norms),
        jnp.zeros_like(conv_wide),
    )
    pieces = (
        lax.all_gather(cached_states.astype(jnp.bfloat16), "group", axis=0, tiled=True).astype(
            jnp.float32
        ),
        lax.all_gather(cached_norms.astype(jnp.bfloat16), "group", axis=0, tiled=True).astype(
            jnp.float32
        ),
        lax.all_gather(conv_wide.astype(jnp.bfloat16), "group", axis=0, tiled=True).astype(
            jnp.float32
        ),
    )
    row_count = pieces[0].shape[0]
    inside = (wanted >= 0) & (wanted < row_count)
    row_index = jnp.clip(wanted, 0, row_count - 1)
    fetched_states, fetched_norms, fetched_conv = tuple(
        (
            jnp.where(
                inside.reshape((requests,) + (1,) * (portion.ndim - 1)), portion[row_index], current
            )
            for portion, current in zip(pieces, blanks)
        )
    )
    has_state = (cached_lengths > 0).astype(jnp.float32)[:, None, None]
    start_states = fetched_states * has_state
    start_norms = fetched_norms * has_state
    qk_rows = lax.dynamic_slice_in_dim(
        qk_weight, first_head * feature, heads_here * feature, 1
    ).reshape(2 * heads_here * feature, model_width)
    in_rows = jnp.concatenate([mixer_weight.reshape(3 * columns, model_width), qk_rows], axis=0)
    whole_rows = lax.all_gather(tokens, "tok", axis=0, tiled=True)
    projected = lax.dot_general(
        rms_scale(whole_rows, norm_gains[0]).astype(jnp.bfloat16),
        in_rows,
        (((1,), (1,)), ((), ())),
        preferred_element_type=jnp.float32,
    )
    values = projected[:, :columns].astype(jnp.bfloat16)
    conv_in = projected[:, columns : 2 * columns]
    conv_gate = projected[:, 2 * columns : 3 * columns]
    lengths = new_lengths[0]
    request_ends, segment, member, offset = segment_layout(lengths, all_rows)
    pieces_out = []
    states_out = []
    norm_share = jnp.zeros((requests, phi_size, head_count), jnp.float32)
    for head_slot in range(heads_here):
        query_low = 3 * columns + head_slot * feature
        key_low = 3 * columns + (heads_here + head_slot) * feature
        queries = projected[:, query_low : query_low + feature]
        keys_head = projected[:, key_low : key_low + feature]
        values_head = values[:, head_slot * head_cols : (head_slot + 1) * head_cols]
        state_head = start_states[:, :, head_slot * head_cols : (head_slot + 1) * head_cols]
        norm_head = lax.dynamic_index_in_dim(start_norms, first_head + head_slot, 2, keepdims=False)
        pieces_out.append(
            head_attention(
                queries, keys_head, values_head, state_head, norm_head, segment, member, query_block
            )
        )
        state_next, norm_next = state_update(keys_head, values_head, member, state_head, norm_head)
        states_out.append(state_next)
        head_pick = (jnp.arange(head_count, dtype=jnp.int32) == first_head + head_slot).astype(
            jnp.float32
        )
        norm_share = norm_share + norm_next[:, :, None] * head_pick[None, None, :] * (
            head_cols / head_width
        )
    new_norms = lax.psum(norm_share.astype(jnp.bfloat16), "tok").astype(jnp.float32)
    conv_out, new_cache = short_conv(
        conv_in,
        conv_gate,
        conv_weight,
        fetched_conv,
        cached_lengths,
        lengths,
        request_ends,
        member,
        offset,
    )
    mixer_in = jnp.concatenate([jnp.concatenate(pieces_out, axis=1), conv_out], axis=1)
    out_rows = out_weight.reshape(2 * columns, model_width)
    ffn_units = ffn_weight.shape[1]
    ffn_rows_all = ffn_weight.reshape(2 * ffn_units, model_width)
    mixed_sum = lax.psum(
        jnp.dot(mixer_in, out_rows, preferred_element_type=jnp.float32).astype(jnp.bfloat16), "tok"
    ).astype(jnp.float32)
    residual = whole_rows.astype(jnp.float32) + mixed_sum
    both_parts = lax.dot_general(
        rms_scale(residual, norm_gains[1]).astype(jnp.bfloat16),
        ffn_rows_all,
        (((1,), (1,)), ((), ())),
        preferred_element_type=jnp.float32,
    )
    hidden = (jax.nn.silu(both_parts[:, :ffn_units]) * both_parts[:, ffn_units:]).astype(
        jnp.bfloat16
    )
    residual_own = lax.dynamic_slice_in_dim(residual, tok_now * tok_rows, tok_rows, 0)
    layer_out = (
        residual_own
        + lax.psum_scatter(
            down_term(hidden, down_weight).astype(jnp.bfloat16),
            "tok",
            scatter_dimension=0,
            tiled=True,
        ).astype(jnp.float32)
    ).astype(jnp.bfloat16)
    return (layer_out, jnp.concatenate(states_out, axis=2), new_norms, new_cache)


def solution(mesh):
    in_specs = (
        P(("group", "tok"), None),
        P(),
        P(),
        P(None, "tok", None),
        P(None, "tok"),
        P(None, "tok", None),
        P(None, "tok", None),
        P("tok", None),
        P("group", None, "tok"),
        P("group", None, None),
        P("group", None, "tok"),
        P("group"),
        P("group", None),
        P(),
    )
    out_specs = (
        P(("group", "tok"), None),
        P("group", None, "tok"),
        P("group", None, None),
        P("group", None, "tok"),
    )
    return jax.shard_map(
        on_device, mesh=mesh, in_specs=in_specs, out_specs=out_specs, check_vma=False
    )
```

profile of v0, /device:TPU:8, one launch (start us, length us, event | category | flops | bytes accessed | tf_op | source)
XLA Modules:
  0.0 291.0 jit_solution(12077999915024894070)
XLA Ops:
  8.0 2.8 convert_element_type.112
  11.1 15.4 %all_gather.14 = bf16[32,273,16]{1,2,0:T(8,128)(2,1)S(1)} all-gather(bf16[8,273,16]{1,2,0:T(8,128)(2,1)S(1)} %convert_element_type.115), channel_id=1, replica_groups=mesh['group'=4,'tok'=8] {'group'}, dimensions={0}, use_global_device_ids=true | all-gather | bytes 349440 | tf_op jit(solution)/shard_map/all_gather | solution.py:162
  27.3 13.3 %all_gather.15 = bf16[32,2,224]{2,1,0:T(2,128)(2,1)S(1)} all-gather(bf16[8,2,224]{2,1,0:T(2,128)(2,1)S(1)} %copy-done.19), channel_id=1, replica_groups=mesh['group'=4,'tok'=8] {'group'}, dimensions={0}, use_global_device_ids=true | all-gather | bytes 35840 | tf_op jit(solution)/shard_map/all_gather | solution.py:165
  45.1 1.7 select_reduce_fusion.2
  46.7 2.2 fusion
  49.2 4.3 %fusion.102 = (bf16[512,736]{0,1:T(8,128)(2,1)}, f32[512,736]{0,1:T(8,128)S(1)}) fusion(bf16[64,1792]{1,0:T(8,128)(2,1)S(1)} %bitcast.113, bf16[672,1792]{1,0:T(8,128)(2,1)} %bitcast.121, bf16[512,1792]{1,0:T(8,128)(2,1)S(1)} %copy-done.3, f32[1792]{0:T(1024)S(1)} %get-tuple-element.30, f32[512]{0:T(512)S(1)} %add_rsqrt_fusion.1), kind=kOutput, calls=%fused_computation.174 | convolution fusion | flops 1359888384 | bytes 6743040 | tf_op jit(solution)/shard_map/dot_general | solution.py:188
  54.3 1.9 fusion.101
  57.4 2.0 fusion.103
  63.1 59.1 %all-gather.5.cloned.1.call-done = bf16[32,273,224]{2,0,1:T(8,128)(2,1)} async-done(((bf16[8,273,224]{2,0,1:T(8,128)(2,1)}), bf16[32,273,224]{2,0,1:T(8,128)(2,1)}) %all-gather.5.cloned.1.call-update) | async-done | bytes 3913744 | tf_op jit(solution)/shard_map/all_gather | solution.py:159
  122.3 8.4 %copy.57 = f32[32,273,224]{2,1,0:T(8,128)} copy(bf16[32,273,224]{2,0,1:T(8,128)(2,1)} %all-gather.5.cloned.1.call-done) | data formatting | bytes 11741184 | tf_op jit(solution)/shard_map/convert_element_type | solution.py:159
  130.7 5.8 %gather_fusion = f32[8,273,224]{2,1,0:T(8,128)} fusion(f32[32,273,224]{2,1,0:T(8,128)} %copy.57, s32[1024]{0:T(1024)} %copy-done.21), kind=kCustom, calls=%fused_computation | custom fusion | bytes 3913760 | tf_op jit(solution)/shard_map/gather | solution.py:175
  136.5 1.9 select_multiply_fusion
  138.4 1.6 slice_bitcast_fusion.1
  140.1 1.2 copy.60
  141.3 2.6 reshape.304
  143.9 2.8 dot_general.74
  146.8 5.8 %select_reduce_fusion.4 = f32[512,112]{0,1:T(8,128)} fusion(f32[8,112,273]{1,0,2:T(8,128)} %dot_general.74, pred[512,8]{0,1:T(8,128)(4,1)} %copy-done.17, f32[512,256]{0,1:T(8,128)} %bitcast.112, f32[512,16]{0,1:T(8,128)} %copy-done.16, f32[273]{0:T(512)} %copy-done.13), kind=kOutput, calls=%fused_computation.32 | convolution fusion | flops 1504011264 | bytes 1770052 | tf_op jit(solution)/shard_map/dot_general | solution.py:61
  153.7 2.6 reshape.303
  156.4 2.8 dot_general.68
  159.2 4.9 %select_reduce_fusion.5 = f32[512,112]{0,1:T(8,128)S(1)} fusion(f32[8,112,273]{1,0,2:T(8,128)} %dot_general.68, pred[512,8]{0,1:T(8,128)(4,1)} %copy-done.17, f32[512,256]{0,1:T(8,128)} %bitcast.110, f32[512,16]{0,1:T(8,128)} %copy-done.15, f32[273]{0:T(512)} %copy-done.13), kind=kOutput, calls=%fused_computation.33 | convolution fusion | flops 1504011264 | bytes 1770052 | tf_op jit(solution)/shard_map/dot_general | solution.py:61
  164.1 1.2 fusion.35
  166.5 2.4 convolution_convert_fusion
  169.2 61.9 %all-reduce.5.cloned.1.call-done = (bf16[512,1792]{1,0:T(8,128)(2,1)}, bf16[8,273,16]{1,2,0:T(8,128)(2,1)}) async-done(((bf16[512,1792]{1,0:T(8,128)(2,1)}, bf16[8,273,16]{1,2,0:T(8,128)(2,1)}), (bf16[512,1792]{1,0:T(8,128)(2,1)}, bf16[8,273,16]{1,2,0:T(8,128)(2,1)})) %all-reduce.5.cloned.1.call-update) | async-done | bytes 1904912 | tf_op jit(solution)/shard_map/psum | solution.py:239
  231.1 4.6 %convert_add_fusion = (f32[512,1792]{1,0:T(8,128)}, f32[512]{0:T(512)S(1)}) fusion(bf16[512,1792]{1,0:T(8,128)(2,1)} %all-gather.3.cloned.1.call-done, bf16[512,1792]{1,0:T(8,128)(2,1)} %get-tuple-element.34), kind=kLoop, calls=%fused_computation.3 | loop fusion | flops 4587008 | bytes 7342080 | tf_op jit(solution)/shard_map/add | solution.py:242
  235.7 4.8 %fusion.7 = f32[512,1216]{0,1:T(8,128)S(1)} fusion(bf16[1216,1792]{1,0:T(8,128)(2,1)} %bitcast.120, f32[1792]{0:T(1024)S(1)} %copy-done.20, f32[512]{0:T(512)S(1)} %add_rsqrt_fusion, bf16[512,1792]{1,0:T(8,128)(2,1)S(1)} %copy-done.4, bf16[512,1792]{1,0:T(8,128)(2,1)S(1)} %copy-done.8), kind=kOutput, calls=%fused_computation.23 | convolution fusion | flops 2236874752 | bytes 10527744 | tf_op jit(solution)/shard_map/dot_general | solution.py:243
  240.5 2.9 %convolution_convert_fusion.1 = bf16[512,1792]{1,0:T(8,128)(2,1)} fusion(bf16[608,1792]{1,0:T(8,128)(2,1)S(1)} %copy-done, f32[512,1216]{0,1:T(8,128)S(1)} %fusion.7), kind=kOutput, calls=%fused_computation.16 | convolution fusion | flops 1118470144 | bytes 6504448 | tf_op jit(solution)/shard_map/dot_general | solution.py:114
  244.2 1.7 select_reduce_fusion.1
  247.8 3.9 %fusion.25 = f32[8,273,112]{2,1,0:T(8,128)S(1)} fusion(f32[8,273,224]{2,1,0:T(8,128)} %copy-done.1, f32[512,112]{0,1:T(8,128)S(1)} %get-tuple-element.51, f32[512,8]{0,1:T(8,128)S(1)} %get-tuple-element.59, f32[512,256]{0,1:T(8,128)S(1)} %bitcast.106, f32[512,16]{0,1:T(8,128)S(1)} %get-tuple-element.45, f32[273]{0:T(512)S(1)} %copy-done.14), kind=kOutput, calls=%fused_computation.38 | convolution fusion | flops 1503854464 | bytes 2760772 | tf_op jit(solution)/shard_map/dot_general | solution.py:81
  251.7 2.1 fusion.28
  254.5 2.0 copy.64
  257.3 25.3 %reduce-scatter.2.cloned.1.call-done = bf16[64,1792]{1,0:T(8,128)(2,1)} async-done(((bf16[512,1792]{1,0:T(8,128)(2,1)}), bf16[64,1792]{1,0:T(8,128)(2,1)}) %reduce-scatter.2.cloned.1.call-update) | async-done | bytes 229392 | tf_op jit(solution)/shard_map/reduce_scatter | solution.py:255
  282.6 1.9 add_convert_fusion
  (150 shorter events, 18.7 us)
Async XLA Ops:
  7.2 233.4 %copy-start = (bf16[608,1792]{1,0:T(8,128)(2,1)S(1)}, bf16[608,1792]{1,0:T(8,128)(2,1)}, u32[]{:S(2)}) copy-start(bf16[608,1792]{1,0:T(8,128)(2,1)} %param.21) | copy-start | bytes 6537220
  7.2 39.5 %all-gather.3.cloned.1.call-start = ((), (), s32[]{:S(2)}) async-start(), calls=%async_computation.1 | async-start | bytes 2064384 | tf_op jit(solution)/shard_map/all_gather | solution.py:187
  7.9 3.0 %copy-start.39 = (s32[32,1]{0,1:T(1,128)S(1)}, s32[32,1]{0,1:T(1,128)}, u32[]{:S(2)}) copy-start(s32[32,1]{0,1:T(1,128)} %param.27) | copy-start | bytes 388
  7.9 3.1 %copy-start.37 = (s32[8]{0:T(128)S(1)}, s32[8]{0:T(128)}, u32[]{:S(2)}) copy-start(s32[8]{0:T(128)} %param.25) | copy-start | bytes 100
  7.9 3.2 %copy-start.11 = (f32[8,273,16]{1,2,0:T(8,128)S(1)}, f32[8,273,16]{1,2,0:T(8,128)}, u32[]{:S(2)}) copy-start(f32[8,273,16]{1,2,0:T(8,128)} %param.23) | copy-start | bytes 419332
  7.9 114.3 %all-gather.5.cloned.1.call-start = ((), (), s32[]{:S(2)}) async-start(), calls=%async_computation.2 | async-start | bytes 5591040 | tf_op jit(solution)/shard_map/all_gather | solution.py:159
  10.8 220.3 %all-reduce.5.cloned.1.call-start = ((), (), s32[]{:S(2)}) async-start(), calls=%async_computation.4 | async-start | bytes 3866624 | tf_op jit(solution)/shard_map/psum | solution.py:239
  11.0 32.9 %copy-start.22 = (pred[8]{0:T(512)(128)(4,1)}, pred[8]{0:T(512)(128)(4,1)S(1)}, u32[]{:S(2)}) copy-start(pred[8]{0:T(512)(128)(4,1)S(1)} %compare_and_fusion) | copy-start | bytes 28
  11.1 29.6 %copy-start.21 = (s32[1024]{0:T(1024)}, s32[1024]{0:T(1024)S(1)}, u32[]{:S(2)}) copy-start(s32[1024]{0:T(1024)S(1)} %pad_clamp_fusion) | copy-start | bytes 12292
  11.1 16.1 %copy-start.23 = (f32[8]{0:T(128)}, f32[8]{0:T(128)S(1)}, u32[]{:S(2)}) copy-start(f32[8]{0:T(128)S(1)} %get-tuple-element.66) | copy-start | bytes 100
  11.1 32.9 %copy-start.24 = (f32[8]{0:T(128)}, f32[8]{0:T(128)S(1)}, u32[]{:S(2)}) copy-start(f32[8]{0:T(128)S(1)} %get-tuple-element.68) | copy-start | bytes 100
  26.5 14.7 %copy-start.40 = (s32[1,8]{1,0:T(1,128)S(1)}, s32[1,8]{1,0:T(1,128)}, u32[]{:S(2)}) copy-start(s32[1,8]{1,0:T(1,128)} %param.26) | copy-start | bytes 100
  26.5 15.5 %copy-start.18 = (f32[2,1792]{1,0:T(2,128)S(1)}, f32[2,1792]{1,0:T(2,128)}, u32[]{:S(2)}) copy-start(f32[2,1792]{1,0:T(2,128)} %param.15) | copy-start | bytes 43012
  26.5 16.8 %copy-start.29 = (f32[3,224]{1,0:T(4,128)S(1)}, f32[3,224]{1,0:T(4,128)}, u32[]{:S(2)}) copy-start(f32[3,224]{1,0:T(4,128)} %param.18) | copy-start | bytes 8068
  41.4 19.2 %copy-start.13 = (f32[273]{0:T(512)}, f32[273]{0:T(512)S(1)}, u32[]{:S(2)}) copy-start(f32[273]{0:T(512)S(1)} %pad.18.clone) | copy-start | bytes 3280
  43.9 9.5 %copy-start.17 = (pred[512,8]{0,1:T(8,128)(4,1)}, pred[512,8]{0,1:T(8,128)(4,1)S(1)}, u32[]{:S(2)}) copy-start(pred[512,8]{0,1:T(8,128)(4,1)S(1)} %get-tuple-element.60) | copy-start | bytes 12292
  53.5 2.7 copy-start.16
  53.5 3.2 %copy-start.15 = (f32[512,16]{0,1:T(8,128)}, f32[512,16]{0,1:T(8,128)S(1)}, u32[]{:S(2)}) copy-start(f32[512,16]{0,1:T(8,128)S(1)} %get-tuple-element.43) | copy-start | bytes 98308
  53.7 3.7 %copy-start.9 = (f32[512,16,16]{0,2,1:T(8,128)}, f32[512,16,16]{0,2,1:T(8,128)S(1)}, u32[]{:S(2)}) copy-start(f32[512,16,16]{0,2,1:T(8,128)S(1)} %get-tuple-element.80) | copy-start | bytes 1572868
  53.7 3.7 %copy-start.10 = (f32[512,16,16]{0,2,1:T(8,128)}, f32[512,16,16]{0,2,1:T(8,128)S(1)}, u32[]{:S(2)}) copy-start(f32[512,16,16]{0,2,1:T(8,128)S(1)} %get-tuple-element.79) | copy-start | bytes 1572868
  146.7 5.8 %copy-start.5 = (f32[273,8,112]{2,0,1:T(8,128)S(1)}, f32[273,8,112]{2,0,1:T(8,128)}, u32[]{:S(2)}) copy-start(f32[273,8,112]{2,0,1:T(8,128)} %get-tuple-element.38) | copy-start | bytes 2935300
  159.1 4.9 %copy-start.33 = (f32[512]{0:T(512)S(1)}, f32[512]{0:T(512)}, u32[]{:S(2)}) copy-start(f32[512]{0:T(512)} %add.154) | copy-start | bytes 6148
  159.1 4.9 %copy-start.42 = (bf16[512,512]{0,1:T(8,128)(2,1)S(1)}, bf16[512,512]{0,1:T(8,128)(2,1)}, u32[]{:S(2)}) copy-start(bf16[512,512]{0,1:T(8,128)(2,1)} %get-tuple-element.70) | copy-start | bytes 1572868
  159.1 4.9 %copy-start.44 = (f32[512,112]{0,1:T(8,128)S(1)}, f32[512,112]{0,1:T(8,128)}, u32[]{:S(2)}) copy-start(f32[512,112]{0,1:T(8,128)} %select_reduce_fusion.4) | copy-start | bytes 688132
  159.1 6.2 %copy-start.34 = (f32[512]{0:T(512)S(1)}, f32[512]{0:T(512)}, u32[]{:S(2)}) copy-start(f32[512]{0:T(512)} %add.148) | copy-start | bytes 6148
  159.2 6.2 %copy-start.43 = (bf16[512,512]{0,1:T(8,128)(2,1)S(1)}, bf16[512,512]{0,1:T(8,128)(2,1)}, u32[]{:S(2)}) copy-start(bf16[512,512]{0,1:T(8,128)(2,1)} %get-tuple-element.74) | copy-start | bytes 1572868
  168.9 113.7 %reduce-scatter.2.cloned.1.call-start = ((), (), s32[]{:S(2)}) async-start(), calls=%async_computation.3 | async-start | bytes 2064384 | tf_op jit(solution)/shard_map/reduce_scatter | solution.py:255
  231.1 4.6 %copy-start.4 = (bf16[512,1792]{1,0:T(8,128)(2,1)S(1)}, bf16[512,1792]{1,0:T(8,128)(2,1)}, u32[]{:S(2)}) copy-start(bf16[512,1792]{1,0:T(8,128)(2,1)} %all-gather.3.cloned.1.call-done) | copy-start | bytes 5505028
  231.1 4.6 %copy-start.8 = (bf16[512,1792]{1,0:T(8,128)(2,1)S(1)}, bf16[512,1792]{1,0:T(8,128)(2,1)}, u32[]{:S(2)}) copy-start(bf16[512,1792]{1,0:T(8,128)(2,1)} %get-tuple-element.34) | copy-start | bytes 5505028
  231.1 4.6 %copy-start.20 = (f32[1792]{0:T(1024)S(1)}, f32[1792]{0:T(1024)}, u32[]{:S(2)}) copy-start(f32[1792]{0:T(1024)} %get-tuple-element.31) | copy-start | bytes 21508
  243.5 4.3 %copy-start.14 = (f32[273]{0:T(512)S(1)}, f32[273]{0:T(512)}, u32[]{:S(2)}) copy-start(f32[273]{0:T(512)} %copy-done.13) | copy-start | bytes 3280
  246.7 5.1 %copy-start.2 = (f32[8,273,224]{2,1,0:T(8,128)S(1)}, f32[8,273,224]{2,1,0:T(8,128)}, u32[]{:S(2)}) copy-start(f32[8,273,224]{2,1,0:T(8,128)} %copy-done.1) | copy-start | bytes 5870596
  (17 other events, 34.0 us)
Sparse Core Ops, SparseCore 0:
  9.9 27.9 all-gather.2
  40.0 82.1 all-gather.4
  169.0 61.9 all-reduce.4
  243.6 38.8 reduce-scatter.1
where the time goes:
time: 293 us; the launch traced here: 291 us
  waiting for transfers between devices  147 us (50%)
  matrix products  39.5 us (13%)
  local copies, waits for them, and re-layouts  36.1 us (12%)
  blocking collectives  28.6 us (10%)
  other arithmetic  24.8 us (8%)
  between operations  14.5 us (5%)
    psum x1, waiting for transfers between devices, on_device(): lax.psum(jnp.dot(mixer_in, out_rows, preferred_element_type=jnp.float32)....  61.9 us
    all_gather x1, waiting for transfers between devices, on_device(): lax.all_gather(cached_states.astype(jnp.bfloat16), 'group', axis=0, tiled...  59.1 us
    reduce_scatter x1, waiting for transfers between devices, on_device(): lax.psum_scatter(down_term(hidden, down_weight).astype(jnp.bfloat16), 'to...  25.3 us
    all_gather x1, blocking collectives, on_device(): lax.all_gather(cached_norms.astype(jnp.bfloat16), 'group', axis=0, tiled=...  15.4 us
    all_gather x1, blocking collectives, on_device(): lax.all_gather(conv_wide.astype(jnp.bfloat16), 'group', axis=0, tiled=True)  13.3 us
    dot_general x2, matrix products, head_attention(): jnp.dot(features, state_flat, precision=highest)  10.6 us
    convert_element_type x1, local copies, waits for them, and re-layouts, on_device(): lax.all_gather(cached_states.astype(jnp.bfloat16), 'group', axis=0, tiled...  8.41 us
    gather x3, local copies, waits for them, and re-layouts, on_device(): portion[row_index]  6.92 us
  transfers between devices with their start and end apart: 4, of which 3 were waited for; matrix products, arithmetic and copies ran while one was open for 13% of the time, Pallas kernels for 0%

commit v1 on v0

--- a/solution.py
+++ b/solution.py
@@ -2,7 +2,10 @@
 
 import jax
 import jax.numpy as jnp
+import numpy as np
 from jax import lax
+from jax.experimental import pallas as pl
+from jax.experimental.pallas import tpu as pltpu
 from jax.sharding import PartitionSpec as P
 
 epsilon = 1e-05
@@ -262,6 +265,586 @@
     return (layer_out, jnp.concatenate(states_out, axis=2), new_norms, new_cache)
 
 
+VMEM = pltpu.VMEM
+wide = 256
+feat_rows = 288
+slot_rows = 304
+big_vmem = 56 * 1024 * 1024
+f32 = jnp.float32
+bf16 = jnp.bfloat16
+
+
+def dot_nt(left, right):
+    return lax.dot_general(left, right, (((1,), (1,)), ((), ())), preferred_element_type=f32)
+
+
+def dot_nn(left, right):
+    return jnp.dot(left, right, preferred_element_type=f32)
+
+
+def feature_tables(heads, feature):
+    parts = 2 * heads
+    first = np.zeros((parts, feature * parts, feat_rows), np.float32)
+    second = np.zeros((parts, feature * parts, feat_rows), np.float32)
+    add = np.zeros((3, feat_rows), np.float32)
+    add[0, 0] = 1.0
+    add[1, : 1 + feature] = 1.0
+    add[2, 0] = 1.0
+    add[2, 1 : 1 + feature] = 0.5
+    add[2, 1 + feature : 1 + feature + feature * feature] = quad_scale
+    for part in range(parts):
+        for a in range(feature):
+            first[part, part * feature + a, 1 + a] = 1.0
+            for b in range(feature):
+                entry = 1 + feature + a * feature + b
+                first[part, part * feature + a, entry] = 1.0
+                second[part, part * feature + b, entry] = 1.0
+    return first, second, add
+
+
+def places():
+    me = lax.axis_index("tok")
+    core = me % 2
+    x = (me // 2) % 2
+    y = me // 4
+    sib = me + 1 - 2 * core
+    xn = me + 2 - 4 * x
+    yn = me + 4 - 8 * y
+    dg = xn + 4 - 8 * y
+    return me, core, sib, (me, xn, yn, dg)
+
+
+def enter():
+    me = lax.axis_index("tok")
+    barrier = pltpu.get_barrier_semaphore()
+    for step in range(1, 8):
+        pl.semaphore_signal(
+            barrier,
+            inc=1,
+            device_id={"tok": (me + step) % 8},
+            device_id_type=pl.DeviceIdType.MESH,
+        )
+    pl.semaphore_wait(barrier, 7)
+
+
+def remote(src, dst, send, recv, target):
+    return pltpu.make_async_remote_copy(
+        src_ref=src,
+        dst_ref=dst,
+        send_sem=send,
+        recv_sem=recv,
+        device_id={"tok": target},
+        device_id_type=pl.DeviceIdType.MESH,
+    )
+
+
+def block_at(ref, index, rows):
+    return ref.at[pl.ds(pl.multiple_of(index * rows, rows), rows)]
+
+
+def gather_rows(own_ref, all_ref, rows, send, recv):
+    me, core, sib, peers = places()
+    home = block_at(all_ref, me, rows)
+    out = []
+    for k in (3, 1, 2):
+        copy = remote(own_ref, home, send.at[k], recv.at[k], peers[k])
+        copy.start()
+        out.append(copy)
+    copy = remote(own_ref, home, send.at[4], recv.at[4], sib)
+    copy.start()
+    out.append(copy)
+    for k in (1, 2, 3):
+        landed = block_at(all_ref, peers[k], rows)
+        remote(own_ref, landed, send.at[k], recv.at[k], peers[k]).wait_recv()
+        copy = remote(landed, landed, send.at[4 + k], recv.at[4 + k], sib)
+        copy.start()
+        out.append(copy)
+    for k in range(4):
+        other = peers[k] + 1 - 2 * core
+        landed = block_at(all_ref, other, rows)
+        remote(landed, landed, send.at[4 + k], recv.at[4 + k], sib).wait_recv()
+    for copy in out:
+        copy.wait_send()
+
+
+def scatter_sum(part_ref, sib_ref, pair_ref, far_ref, rows, send, recv):
+    me, core, sib, peers = places()
+    out = []
+    for k in (3, 1, 2, 0):
+        theirs = peers[k] + 1 - 2 * core
+        copy = remote(block_at(part_ref, theirs, rows), sib_ref.at[k], send.at[k], recv.at[k], sib)
+        copy.start()
+        out.append(copy)
+    for place, k in enumerate((3, 1, 2)):
+        out[place].wait_recv()
+        pair_ref[k] = (
+            block_at(part_ref, peers[k], rows)[...].astype(f32) + sib_ref[k].astype(f32)
+        ).astype(bf16)
+        copy = remote(pair_ref.at[k], far_ref.at[k], send.at[4 + k], recv.at[4 + k], peers[k])
+        copy.start()
+        out.append(copy)
+    out[3].wait_recv()
+    total = block_at(part_ref, me, rows)[...].astype(f32) + sib_ref[0].astype(f32)
+    for place, k in enumerate((3, 1, 2)):
+        out[4 + place].wait_recv()
+    for k in (1, 2, 3):
+        total = total + far_ref[k].astype(f32)
+    for copy in out:
+        copy.wait_send()
+    return total
+
+
+def token_kernel(own_ref, all_ref, held, send, recv, local):
+    rows = own_ref.shape[0]
+    enter()
+    me = lax.axis_index("tok")
+    copy = pltpu.make_async_copy(own_ref, block_at(held, me, rows), local)
+    copy.start()
+    gather_rows(own_ref, held, rows, send, recv)
+    copy.wait()
+    all_ref[...] = held[...]
+
+
+def pick_kernel(slot_ref, state_ref, norm_ref, conv_ref, out_ref):
+    phi_size, columns = state_ref.shape[1], state_ref.shape[2]
+    head_count = norm_ref.shape[2]
+    heads = slot_ref[8]
+    row = lax.broadcasted_iota(jnp.int32, (head_count, wide), 0)
+    col = lax.broadcasted_iota(jnp.int32, (head_count, wide), 1)
+    choose = ((col >= columns) & (col < columns + 2) & (row == heads + col - columns)).astype(f32)
+    out_ref[0] = jnp.zeros((slot_rows, wide), bf16)
+    out_ref[0, 0:phi_size, :] = dot_nn(
+        norm_ref[0].astype(bf16), choose.astype(bf16)
+    ).astype(bf16)
+    out_ref[0, 0:phi_size, 0:columns] = state_ref[0].astype(bf16)
+    out_ref[0, feat_rows : feat_rows + 2, 0:columns] = conv_ref[0]
+
+
+def head_zero(shape, columns):
+    col = lax.broadcasted_iota(jnp.int32, shape, 1)
+    return (col < columns // 2) | (col == columns)
+
+
+def local_kernel(
+    info_ref, rows_ref, gain_ref, mixer_ref, qk_ref, qk_out, v_out, conv_out, gate_out, acc_out, normed
+):
+    all_rows = rows_ref.shape[0]
+    columns = mixer_ref.shape[1]
+    feature = 16
+    half = 256
+
+    @pl.loop(0, all_rows // half)
+    def _(step):
+        span = pl.ds(pl.multiple_of(step * half, half), half)
+        x = rows_ref[span, :].astype(f32)
+        scale = lax.rsqrt(jnp.mean(x * x, axis=-1, keepdims=True) + epsilon)
+        normed[...] = (x * scale * gain_ref[0:1, :]).astype(bf16)
+        v_out[span, :] = jnp.ones((half, wide), bf16)
+        v_out[span, 0:columns] = dot_nt(normed[...], mixer_ref[0]).astype(bf16)
+        conv_out[span, :] = dot_nt(normed[...], mixer_ref[1])
+        gate_out[span, :] = dot_nt(normed[...], mixer_ref[2])
+        qk_out[span, :] = dot_nt(normed[...], qk_ref[...].reshape(4 * feature, qk_ref.shape[2]))
+
+    block = 128
+
+    @pl.loop(0, all_rows // block)
+    def _(step):
+        low = pl.multiple_of(step * block, block)
+        span = pl.ds(low, block)
+        query = qk_out[span, :]
+        i = lax.broadcasted_iota(jnp.int32, (block, 1), 0) + low
+        begin = jnp.zeros((block, 1), jnp.int32)
+        for r in range(8):
+            begin = jnp.where(i >= info_ref[r], info_ref[r], begin)
+        j = lax.broadcasted_iota(jnp.int32, (block, all_rows), 1)
+        allowed = (j <= i) & (j >= begin)
+        found = []
+        for h in range(2):
+            q = query[:, h * feature : (h + 1) * feature].astype(bf16)
+            k = qk_out[:, (2 + h) * feature : (3 + h) * feature].astype(bf16)
+            s = dot_nt(q, k)
+            w = jnp.where(allowed, 1.0 + 0.25 * s + s * s * (1.0 / 32.0), 0.0).astype(bf16)
+            found.append(dot_nn(w, v_out[...]))
+        acc_out[span, :] = jnp.where(head_zero((block, wide), columns), found[0], found[1])
+
+
+def carried_kernel(
+    info_ref,
+    qk_ref,
+    v_ref,
+    conv_ref,
+    gate_ref,
+    acc_ref,
+    slots_a,
+    slots_b,
+    slots_c,
+    slots_d,
+    first_ref,
+    second_ref,
+    add_ref,
+    first_t_ref,
+    second_t_ref,
+    add_t_ref,
+    taps_ref,
+    weight_ref,
+    mixed_out,
+    state_out,
+    norm_out,
+    cache_out,
+    num,
+    shifted,
+    prev_one,
+    prev_two,
+    phi_q,
+    phi_k,
+    att,
+):
+    all_rows, columns = conv_ref.shape
+    phi_size = state_out.shape[1]
+    hi = qk_ref[...].astype(bf16)
+    lo = (qk_ref[...] - hi.astype(f32)).astype(bf16)
+    for h in range(2):
+        one = dot_nn(hi, first_ref[h]) + dot_nn(lo, first_ref[h]) + add_ref[0:1]
+        two = dot_nn(hi, second_ref[h]) + dot_nn(lo, second_ref[h]) + add_ref[1:2]
+        phi_q[h] = (one * two * add_ref[2:3]).astype(bf16)
+        one = dot_nt(first_t_ref[h], hi) + dot_nt(first_t_ref[h], lo) + add_t_ref[:, 0:1]
+        two = dot_nt(second_t_ref[h], hi) + dot_nt(second_t_ref[h], lo) + add_t_ref[:, 1:2]
+        phi_k[h] = (one * two * add_t_ref[:, 2:3]).astype(bf16)
+    num[...] = acc_ref[...]
+    shifted[0:8, :] = jnp.zeros((8, columns), f32)
+    shifted[8 : 8 + all_rows, :] = conv_ref[...]
+    prev_one[...] = shifted[7 : 7 + all_rows, :]
+    prev_two[...] = shifted[6 : 6 + all_rows, :]
+    i = lax.broadcasted_iota(jnp.int32, (all_rows, 1), 0)
+    row_zero = head_zero((all_rows, wide), columns)
+    state_zero = head_zero((feat_rows, wide), columns)
+    for index in range(8):
+        slots = (slots_a, slots_b, slots_c, slots_d)[index // 2]
+        request = info_ref[24 + index]
+        begin = info_ref[request]
+        length = info_ref[8 + request]
+        cached = info_ref[16 + request]
+        end = begin + length
+        live = jnp.where(cached > 0, 1.0, 0.0).astype(f32)
+        state = slots[index % 2, 0:feat_rows, :]
+        member = (i >= begin) & (i < end)
+        carried = jnp.where(row_zero, dot_nn(phi_q[0], state), dot_nn(phi_q[1], state)) * live
+        num[...] += jnp.where(member, carried, 0.0)
+        mine = jnp.where(member, v_ref[...].astype(f32), 0.0).astype(bf16)
+        added = jnp.where(state_zero, dot_nn(phi_k[0], mine), dot_nn(phi_k[1], mine))
+        fresh = state.astype(f32) * live + added
+        state_out[request] = fresh[0:phi_size, 0:columns]
+        norm_out[request] = fresh[0:feat_rows, 128:256]
+        tail = slots[index % 2, feat_rows:slot_rows, 0:columns].astype(f32)
+        newest = tail[1:2] * live
+        oldest = tail[0:1] * jnp.where(cached >= 2, 1.0, 0.0).astype(f32)
+        prev_one[...] = jnp.where(i == begin, newest, prev_one[...])
+        prev_two[...] = jnp.where(
+            i == begin, oldest, jnp.where((i == begin + 1) & (i < end), newest, prev_two[...])
+        )
+        final = shifted[pl.ds(7 + end, 1), :]
+        before = shifted[pl.ds(6 + end, 1), :]
+        cache_out[request, 0:1, :] = jnp.where(length >= 2, before, newest)
+        cache_out[request, 1:2, :] = final
+    col = lax.broadcasted_iota(jnp.int32, (all_rows, wide), 1)
+    den = jnp.where(col < columns // 2, num[:, columns : columns + 1], num[:, columns + 1 : columns + 2])
+    att[...] = (num[...] / den).astype(bf16)
+    convolved = (
+        taps_ref[0:1] * conv_ref[...] + taps_ref[1:2] * prev_one[...] + taps_ref[2:3] * prev_two[...]
+    )
+    gated = (convolved * gate_ref[...]).astype(bf16)
+    prev_one[...] = gated.astype(f32)
+
+    @pl.loop(0, all_rows // 256)
+    def _(step):
+        span = pl.ds(pl.multiple_of(step * 256, 256), 256)
+        mixed_out[span, :] = (
+            dot_nn(att[span, 0:columns], weight_ref[0])
+            + dot_nn(prev_one[span, :].astype(bf16), weight_ref[1])
+        ).astype(bf16)
+
+
+def ffn_kernel(
+    part_ref,
+    own_ref,
+    gain_ref,
+    norm_ref,
+    up_hbm,
+    down_hbm,
+    out_ref,
+    norms_out,
+    up,
+    down,
+    sib_a,
+    pair_a,
+    far_a,
+    sib_b,
+    pair_b,
+    far_b,
+    own_normed,
+    normed,
+    part_two,
+    norms,
+    send_a,
+    recv_a,
+    send_b,
+    recv_b,
+    send_g,
+    recv_g,
+    send_n,
+    recv_n,
+    load,
+):
+    rows = own_ref.shape[0]
+    all_rows = part_ref.shape[0]
+    up_copy = pltpu.make_async_copy(up_hbm, up, load.at[0])
+    down_copy = pltpu.make_async_copy(down_hbm, down, load.at[1])
+    up_copy.start()
+    down_copy.start()
+    enter()
+    me = lax.axis_index("tok")
+    small = []
+    total = scatter_sum(part_ref, sib_a, pair_a, far_a, rows, send_a, recv_a)
+    residual = own_ref[...].astype(f32) + total
+    scale = lax.rsqrt(jnp.mean(residual * residual, axis=-1, keepdims=True) + epsilon)
+    own_normed[...] = (residual * scale * gain_ref[1:2, :]).astype(bf16)
+    mine = pltpu.make_async_copy(own_normed, block_at(normed, me, rows), load.at[2])
+    mine.start()
+    gather_rows(own_normed, normed, rows, send_g, recv_g)
+    for step in range(1, 8):
+        copy = remote(
+            norm_ref, norms.at[me], send_n.at[step - 1], recv_n.at[step - 1], (me + step) % 8
+        )
+        copy.start()
+        small.append(copy)
+    norms[me] = norm_ref[...]
+    mine.wait()
+    up_copy.wait()
+    down_copy.wait()
+    half = 256
+
+    @pl.loop(0, all_rows // half)
+    def _(step):
+        span = pl.ds(pl.multiple_of(step * half, half), half)
+        gate = dot_nt(normed[span, :], up[0])
+        lift = dot_nt(normed[span, :], up[1])
+        hidden = (gate / (1.0 + jnp.exp(-gate)) * lift).astype(bf16)
+        part_two[span, :] = dot_nn(hidden, down[...]).astype(bf16)
+
+    total = scatter_sum(part_two, sib_b, pair_b, far_b, rows, send_b, recv_b)
+    out_ref[...] = (residual + total).astype(bf16)
+    for step in range(1, 8):
+        small[step - 1].wait_send()
+        remote(
+            norm_ref,
+            norms.at[(me + 8 - step) % 8],
+            send_n.at[step - 1],
+            recv_n.at[step - 1],
+            (me + step) % 8,
+        ).wait_recv()
+    norms_out[...] = norms[...]
+
+
+def fast_device(
+    tokens,
+    norm_gains,
+    qk_weight,
+    mixer_weight,
+    conv_weight,
+    out_weight,
+    ffn_weight,
+    down_weight,
+    cached_states,
+    cached_norms,
+    conv_cache,
+    cached_lengths,
+    new_lengths,
+    state_source,
+):
+    rows, width = tokens.shape
+    all_rows = 8 * rows
+    requests, phi_size, columns = cached_states.shape
+    head_count = cached_norms.shape[2]
+    feature = qk_weight.shape[1] // head_count
+    heads = 2
+    groups = lax.axis_size("group")
+    group_now = lax.axis_index("group")
+    tok_now = lax.axis_index("tok")
+    shape = jax.ShapeDtypeStruct
+    dma = pltpu.SemaphoreType.DMA
+    in_vmem = pl.BlockSpec(memory_space=VMEM)
+    in_smem = pl.BlockSpec(memory_space=pltpu.SMEM)
+
+    sources = state_source[:, 0].reshape(groups, requests)
+    request = jnp.arange(requests, dtype=jnp.int32)
+    shift = jnp.arange(groups, dtype=jnp.int32)
+
+    def ends_of(match):
+        low = jnp.min(jnp.where(match, request[None], requests - 1), axis=1)
+        high = jnp.max(jnp.where(match, request[None], 0), axis=1)
+        return jnp.stack([low, high], axis=1).reshape(-1).astype(jnp.int32)
+
+    give = ends_of(sources[(group_now + shift) % groups] == group_now)
+    own_sources = lax.dynamic_index_in_dim(sources, group_now, 0, keepdims=False)
+    take = ends_of(own_sources[None] == ((group_now + groups - shift) % groups)[:, None])
+    lengths = new_lengths[0]
+    starts = jnp.cumsum(lengths) - lengths
+    info = jnp.concatenate([starts, lengths, cached_lengths, take]).astype(jnp.int32)
+    picks = jnp.concatenate([give, (tok_now * heads)[None].astype(jnp.int32)])
+
+    packed = pl.pallas_call(
+        pick_kernel,
+        grid_spec=pltpu.PrefetchScalarGridSpec(
+            num_scalar_prefetch=1,
+            grid=(2 * groups,),
+            in_specs=[
+                pl.BlockSpec((1, phi_size, columns), lambda i, s: (s[i], 0, 0)),
+                pl.BlockSpec((1, phi_size, head_count), lambda i, s: (s[i], 0, 0)),
+                pl.BlockSpec((1, 2, columns), lambda i, s: (s[i], 0, 0)),
+            ],
+            out_specs=pl.BlockSpec((1, slot_rows, wide), lambda i, s: (i, 0, 0)),
+        ),
+        out_shape=shape((2 * groups, slot_rows, wide), bf16),
+        name="pick_slots",
+    )(picks, cached_states, cached_norms, conv_cache)
+    arrived = [packed[0:2]]
+    for step in range(1, groups):
+        ring = [(g, (g + step) % groups) for g in range(groups)]
+        arrived.append(lax.ppermute(packed[2 * step : 2 * step + 2], "group", ring))
+
+    whole_rows = pl.pallas_call(
+        token_kernel,
+        out_shape=shape((all_rows, width), bf16),
+        in_specs=[in_vmem],
+        out_specs=in_vmem,
+        scratch_shapes=[VMEM((all_rows, width), bf16), dma((8,)), dma((8,)), dma],
+        compiler_params=pltpu.CompilerParams(
+            collective_id=0, has_side_effects=True, vmem_limit_bytes=big_vmem
+        ),
+        cost_estimate=pl.CostEstimate(flops=0, bytes_accessed=30000000, transcendentals=0),
+        name="gather_tokens",
+    )(tokens)
+
+    def full(*dims):
+        return pl.BlockSpec(dims, lambda i, s: (0,) * len(dims))
+
+    tok_pick = jnp.concatenate([info, tok_now[None].astype(jnp.int32)])
+    qk, vext, conv_in, gate, acc = pl.pallas_call(
+        local_kernel,
+        grid_spec=pltpu.PrefetchScalarGridSpec(
+            num_scalar_prefetch=1,
+            grid=(1,),
+            in_specs=[
+                full(all_rows, width),
+                full(2, width),
+                full(3, columns, width),
+                pl.BlockSpec((2, heads * feature, width), lambda i, s: (0, s[32], 0)),
+            ],
+            out_specs=[
+                full(all_rows, 4 * feature),
+                full(all_rows, wide),
+                full(all_rows, columns),
+                full(all_rows, columns),
+                full(all_rows, wide),
+            ],
+            scratch_shapes=[VMEM((256, width), bf16)],
+        ),
+        out_shape=[
+            shape((all_rows, 4 * feature), f32),
+            shape((all_rows, wide), bf16),
+            shape((all_rows, columns), f32),
+            shape((all_rows, columns), f32),
+            shape((all_rows, wide), f32),
+        ],
+        compiler_params=pltpu.CompilerParams(vmem_limit_bytes=big_vmem),
+        cost_estimate=pl.CostEstimate(flops=2000000000, bytes_accessed=30000000, transcendentals=0),
+        name="local_attention",
+    )(tok_pick, whole_rows, norm_gains, mixer_weight, qk_weight)
+
+    first, second, add = feature_tables(heads, feature)
+    mixed, new_states, norm_wide, cache_next = pl.pallas_call(
+        carried_kernel,
+        in_specs=[in_smem] + [in_vmem] * 17,
+        out_specs=[in_vmem] * 4,
+        out_shape=[
+            shape((all_rows, width), bf16),
+            shape((requests, phi_size, columns), f32),
+            shape((requests, feat_rows, 128), f32),
+            shape((requests, 2, columns), f32),
+        ],
+        scratch_shapes=[
+            VMEM((all_rows, wide), f32),
+            VMEM((all_rows + 8, columns), f32),
+            VMEM((all_rows, columns), f32),
+            VMEM((all_rows, columns), f32),
+            VMEM((2, all_rows, feat_rows), bf16),
+            VMEM((2, feat_rows, all_rows), bf16),
+            VMEM((all_rows, wide), bf16),
+        ],
+        compiler_params=pltpu.CompilerParams(vmem_limit_bytes=big_vmem),
+        name="carried_states",
+    )(
+        info,
+        qk,
+        vext,
+        conv_in,
+        gate,
+        acc,
+        *arrived,
+        jnp.asarray(first[:heads], bf16),
+        jnp.asarray(second[:heads], bf16),
+        jnp.asarray(add, f32),
+        jnp.asarray(first[heads:].transpose(0, 2, 1), bf16),
+        jnp.asarray(second[heads:].transpose(0, 2, 1), bf16),
+        jnp.asarray(add.T, f32),
+        conv_weight,
+        out_weight,
+    )
+    low = columns - 128
+    share = norm_wide[:, :, low : low + heads].astype(bf16)
+    share = jnp.transpose(share, (2, 0, 1)).reshape(heads * requests, feat_rows)
+    share = jnp.pad(share, ((0, 0), (0, 384 - feat_rows)))
+
+    units = ffn_weight.shape[1]
+    blocks = VMEM((4, rows, width), bf16)
+    in_any = pl.BlockSpec(memory_space=pl.ANY)
+    layer_out, norms = pl.pallas_call(
+        ffn_kernel,
+        in_specs=[in_vmem, in_vmem, in_vmem, in_vmem, in_any, in_any],
+        out_specs=[in_vmem, in_vmem],
+        out_shape=[shape((rows, width), bf16), shape((8,) + share.shape, bf16)],
+        scratch_shapes=[
+            VMEM((2, units, width), bf16),
+            VMEM((units, width), bf16),
+            blocks,
+            blocks,
+            blocks,
+            blocks,
+            blocks,
+            blocks,
+            VMEM((rows, width), bf16),
+            VMEM((all_rows, width), bf16),
+            VMEM((all_rows, width), bf16),
+            VMEM((8,) + share.shape, bf16),
+        ]
+        + [dma((8,))] * 8
+        + [dma((3,))],
+        compiler_params=pltpu.CompilerParams(
+            collective_id=1, has_side_effects=True, vmem_limit_bytes=big_vmem
+        ),
+        name="sum_and_ffn",
+    )(mixed, tokens, norm_gains, share, ffn_weight, down_weight)
+    norms = norms.reshape(8, heads, requests, -1)[:, :, :, :phi_size].astype(f32)
+    new_norms = jnp.transpose(norms, (2, 3, 0, 1)).reshape(requests, phi_size, head_count)
+    return (layer_out, new_states, new_norms, cache_next.astype(bf16))
+
+
+def device_function(mesh):
+    if dict(mesh.shape) == {"group": 4, "tok": 8}:
+        return fast_device
+    return on_device
+
+
 def solution(mesh):
     in_specs = (
         P(("group", "tok"), None),
@@ -286,5 +869,5 @@
         P("group", None, "tok"),
     )
     return jax.shard_map(
-        on_device, mesh=mesh, in_specs=in_specs, out_specs=out_specs, check_vma=False
-    )
+        device_function(mesh), mesh=mesh, in_specs=in_specs, out_specs=out_specs, check_vma=False
+    )

time: 293 us -> 127 us (0.43)
  waiting for transfers between devices: 147 us -> 0.01 us
  Pallas kernels: 0 us -> 96.8 us
  matrix products: 39.5 us -> 0 us
  blocking collectives: 28.6 us -> 0 us
  other arithmetic: 24.8 us -> 5.3 us
  local copies, waits for them, and re-layouts: 36.1 us -> 17.1 us
  between operations: 14.5 us -> 0.73 us
  starting transfers between devices: 0.38 us -> 5.57 us
    pallas_call x0 -> x5, Pallas kernels: none -> 96.8 us  [the longest x1 51.4 us: fast_device(): pl.pallas_call(ffn_kernel, in_specs=[in_vmem, in_vmem, in_vmem, in_vmem,...]
    psum x1 -> x0, waiting for transfers between devices: 61.9 us -> none  [on_device(): lax.psum(jnp.dot(mixer_in, out_rows, preferred_element_type=jnp.float32)....]
    all_gather x2 -> x0, waiting for transfers between devices: 59.1 us -> none  [the longest x1 59.1 us: on_device(): lax.all_gather(cached_states.astype(jnp.bfloat16), 'group', axis=0, tiled...]
    dot_general x16 -> x0, matrix products: 39.5 us -> none  [the longest x2 10.6 us: head_attention(): jnp.dot(features, state_flat, precision=highest)]
    all_gather x2 -> x0, blocking collectives: 28.6 us -> none  [the longest x1 15.4 us: on_device(): lax.all_gather(cached_norms.astype(jnp.bfloat16), 'group', axis=0, tiled=...]
    reduce_scatter x1 -> x0, waiting for transfers between devices: 25.3 us -> none  [on_device(): lax.psum_scatter(down_term(hidden, down_weight).astype(jnp.bfloat16), 'to...]
    convert_element_type x1 -> x0, local copies, waits for them, and re-layouts: 8.41 us -> none  [on_device(): lax.all_gather(cached_states.astype(jnp.bfloat16), 'group', axis=0, tiled...]
    unnamed x91 -> x19, local copies, waits for them, and re-layouts: 3.6 us -> 10.3 us
  transfers between devices with their start and end apart: 4 -> 3, of which waited for: 3 -> 0; matrix products, arithmetic and copies ran while one was open for 13% -> 1% of each run, Pallas kernels for 0% -> 21%
where the time goes in v1:
time: 127 us; the launch traced here: 125 us
  Pallas kernels  96.8 us (76%)
  local copies, waits for them, and re-layouts  17.1 us (13%)
  starting transfers between devices  5.57 us (4%)
  other arithmetic  5.3 us (4%)
    pallas_call x1, Pallas kernels, fast_device(): pl.pallas_call(ffn_kernel, in_specs=[in_vmem, in_vmem, in_vmem, in_vmem,...  51.4 us
    pallas_call x1, Pallas kernels, fast_device(): pl.pallas_call(token_kernel, out_shape=shape((all_rows, width), bf16), in...  18.4 us
    pallas_call x1, Pallas kernels, fast_device(): pl.pallas_call(carried_kernel, in_specs=[in_smem] + [in_vmem] * 17, out_s...  11.6 us
    unnamed x19, local copies, waits for them, and re-layouts  10.3 us
    pallas_call x1, Pallas kernels, fast_device(): pl.pallas_call(local_kernel, grid_spec=pltpu.PrefetchScalarGridSpec(num_s...  8.34 us
    pallas_call x1, Pallas kernels, fast_device(): pl.pallas_call(pick_kernel, grid_spec=pltpu.PrefetchScalarGridSpec(num_sc...  7.06 us
    ppermute x3, starting transfers between devices, fast_device(): arrived.append(lax.ppermute(packed[2 * step:2 * step + 2], 'group', ring))  5.57 us
  transfers between devices with their start and end apart: 3, of which 0 were waited for; matrix products, arithmetic and copies ran while one was open for 1% of the time, Pallas kernels for 21%

profile of v1, /device:TPU:8, one launch (start us, length us, event | category | flops | bytes accessed | tf_op | source)
XLA Modules:
  0.0 125.5 jit_solution(16455809594488343883)
XLA Ops:
  0.7 0.5 broadcast.104
  1.2 1.3 %reduce.3 = s32[32]{0:T(128)S(1)} reduce(s32[32,1]{0,1:T(1,128)} %param.33, s32[]{:T(128)} %broadcast.104), dimensions={1}, to_apply=%param.33.reduce_sub_computation.3 | reduce | bytes 260 | tf_op args[13]
  2.6 0.6 gather_fusion
  3.1 0.2 select_reduce_fusion.1
  3.3 0.1 copy.32
  3.5 2.3 %copy.34.norm_ref = f32[8,273,16]{2,1,0:T(8,128)} copy(f32[8,273,16]{1,2,0:T(8,128)} %param.29) | data formatting | bytes 279552 | tf_op args[9]
  5.8 3.7 %copy.33.state_ref = f32[8,273,224]{2,1,0:T(8,128)} copy(f32[8,273,224]{2,0,1:T(8,128)} %param.28) | data formatting | bytes 3913728 | tf_op args[8]
  9.5 0.6 pad_add_fusion.3.slot_ref
  10.1 7.1 %pick_slots.1 = bf16[8,304,256]{2,1,0:T(8,128)(2,1)} custom-call(s32[9]{0:T(128)} %pad_add_fusion.3.slot_ref, f32[8,273,224]{2,1,0:T(8,128)} %copy.33.state_ref, f32[8,273,16]{2,1,0:T(8,128)} %copy.34.norm_ref, bf16[8,2,224]{2,1,0:T(2,128)(2,1)} %conv_ref.1), custom_call_target="tpu_custom_call" | custom-call | tf_op jit(solution)/shard_map/pick_slots/pallas_call | solution.py:695
  17.2 2.1 %fusion.6 = (bf16[2,304,256]{2,1,0:T(8,128)(2,1)S(1)}, bf16[2,304,256]{2,1,0:T(8,128)(2,1)S(1)}, bf16[2,304,256]{2,1,0:T(8,128)(2,1)S(1)}, bf16[2,304,256]{2,1,0:T(8,128)(2,1)}) fusion(bf16[8,304,256]{2,1,0:T(8,128)(2,1)} %pick_slots.1), kind=kLoop, calls=%fused_computation.28 | loop fusion | bytes 2490368 | tf_op jit(solution)/shard_map/slice | solution.py:713
  19.3 3.0 %collective-permute-start.1 = (bf16[2,304,256]{2,1,0:T(8,128)(2,1)S(1)}, bf16[2,304,256]{2,1,0:T(8,128)(2,1)S(1)}, u32[]{:S(2)}, u32[]{:S(2)}) collective-permute-start(bf16[2,304,256]{2,1,0:T(8,128)(2,1)S(1)} %get-tuple-element.39), channel_id=1, source_target_pairs={{0,16},{8,24},{16,0},{24,8},{1,17},{9,25},{17,1},{25,9},{2,18},{10... | collective-permute-start | bytes 933896 | tf_op jit(solution)/shard_map/ppermute | solution.py:713
  22.3 2.5 %collective-permute-start = (bf16[2,304,256]{2,1,0:T(8,128)(2,1)S(1)}, bf16[2,304,256]{2,1,0:T(8,128)(2,1)S(1)}, u32[]{:S(2)}, u32[]{:S(2)}) collective-permute-start(bf16[2,304,256]{2,1,0:T(8,128)(2,1)S(1)} %get-tuple-element.40), channel_id=1, source_target_pairs={{0,8},{8,16},{16,24},{24,0},{1,9},{9,17},{17,25},{25,1},{2,10},{10... | collective-permute-start | bytes 933896 | tf_op jit(solution)/shard_map/ppermute | solution.py:713
  24.8 0.2 reduce-window.9
  25.0 0.2 fusion.1
  25.2 0.1 copy.31
  25.4 18.4 %gather_tokens.1.rows_ref = bf16[512,1792]{1,0:T(8,128)(2,1)} custom-call(bf16[64,1792]{1,0:T(8,128)(2,1)} %own_ref.3), custom_call_target="tpu_custom_call" | custom-call | bytes 30000000 | tf_op jit(solution)/shard_map/gather_tokens/pallas_call | solution.py:715
  43.8 0.6 concatenate.11.info_ref
  44.4 0.6 pad_add_fusion.2.info_ref
  45.0 8.3 %local_attention.1 = (f32[512,64]{1,0:T(8,128)}, bf16[512,256]{1,0:T(8,128)(2,1)}, f32[512,224]{1,0:T(8,128)}, f32[512,224]{1,0:T(8,128)}, f32[512,256]{1,0:T(8,128)}) custom-call(s32[33]{0:T(128)} %concatenate.11.info_ref, bf16[512,1792]{1,0:T(8,128)(2,1)} %gather_tokens.1.rows_ref, f32[2,1792]{1,0:T(2,128)} %gain_ref.3, bf16[3,224,1792]{2,1,0:T(8,128)(2,1)} %mixer_ref.1, ...), custom_call_target="tpu_custom_call" | custom-call | flops 2000000000 | bytes 30000000 | tf_op jit(solution)/shard_map/local_attention/pallas_call | solution.py:732
  53.4 0.7 copy-done.1
  54.1 0.1 copy-done.2
  54.2 0.1 copy-done.3
  54.3 11.6 %carried_states.1 = (bf16[512,1792]{1,0:T(8,128)(2,1)}, f32[8,273,224]{2,1,0:T(8,128)}, f32[8,288,128]{2,1,0:T(8,128)}, f32[8,2,224]{2,1,0:T(2,128)}) custom-call(s32[32]{0:T(128)} %pad_add_fusion.2.info_ref, f32[512,64]{1,0:T(8,128)} %get-tuple-element.15.qk_ref, bf16[512,256]{1,0:T(8,128)(2,1)} %get-tuple-element.16.v_ref, ...), custom_call_target="tpu_custom_call" | custom-call | tf_op jit(solution)/shard_map/carried_states/pallas_call | solution.py:765
  65.9 1.3 %convert_element_type.4 = bf16[8,2,224]{2,1,0:T(2,128)(2,1)} convert(f32[8,2,224]{2,1,0:T(2,128)} %get-tuple-element.25) | non-fusion elementwise | flops 3584 | bytes 21504 | tf_op jit(solution)/shard_map/convert_element_type | solution.py:839
  67.3 1.5 %fusion = bf16[2,8,288]{0,2,1:T(8,128)(2,1)S(1)} fusion(f32[8,288,128]{2,1,0:T(8,128)} %get-tuple-element.21), kind=kLoop, calls=%fused_computation.2 | loop fusion | bytes 18432 | tf_op jit(solution)/shard_map/transpose | solution.py:805
  68.8 0.3 copy.35
  69.1 0.6 pad.4.norm_ref
  69.7 51.4 %sum_and_ffn.1 = (bf16[64,1792]{1,0:T(8,128)(2,1)}, bf16[8,16,384]{2,1,0:T(8,128)(2,1)}) custom-call(bf16[512,1792]{1,0:T(8,128)(2,1)} %get-tuple-element.20.part_ref, bf16[64,1792]{1,0:T(8,128)(2,1)} %own_ref.3, f32[2,1792]{1,0:T(2,128)} %gain_ref.3, bf16[16,384]{1,0:T(8,128)(2,1)} %pad.4.norm_ref, bf16[2,608,1792]{2,1,0:T(8,128)(2,1)} %up_hbm.1, ...), custom_call_target="tpu_custom_call" | custom-call | tf_op jit(solution)/shard_map/sum_and_ffn/pallas_call | solution.py:811
  121.1 0.9 slice_convert_fusion.1
  122.0 0.7 copy.38
  122.8 2.0 %copy.37 = f32[8,273,224]{2,0,1:T(8,128)} copy(f32[8,273,224]{2,1,0:T(8,128)S(1)} %copy-done) | data formatting | bytes 3913728
  124.8 0.7 copy.40
  (25 shorter events, 0.3 us)
Async XLA Ops:
  17.2 7.7 %copy-start.6 = (s32[1,8]{1,0:T(1,128)S(1)}, s32[1,8]{1,0:T(1,128)}, u32[]{:S(2)}) copy-start(s32[1,8]{1,0:T(1,128)} %param.32) | copy-start | bytes 100
  17.2 26.6 %copy-start.5 = (s32[8]{0:T(128)S(1)}, s32[8]{0:T(128)}, u32[]{:S(2)}) copy-start(s32[8]{0:T(128)} %param.31) | copy-start | bytes 100
  19.3 34.1 %collective-permute-start.2 = (bf16[2,304,256]{2,1,0:T(8,128)(2,1)S(1)}, bf16[2,304,256]{2,1,0:T(8,128)(2,1)S(1)}, u32[]{:S(2)}, u32[]{:S(2)}) collective-permute-start(bf16[2,304,256]{2,1,0:T(8,128)(2,1)S(1)} %get-tuple-element.38), channel_id=1, source_target_pairs={{0,24},{8,0},{16,8},{24,16},{1,25},{9,1},{17,9},{25,17},{2,26},{10... | collective-permute-start | bytes 933896 | tf_op jit(solution)/shard_map/ppermute | solution.py:713
  19.3 34.1 %collective-permute-start.1 = (bf16[2,304,256]{2,1,0:T(8,128)(2,1)S(1)}, bf16[2,304,256]{2,1,0:T(8,128)(2,1)S(1)}, u32[]{:S(2)}, u32[]{:S(2)}) collective-permute-start(bf16[2,304,256]{2,1,0:T(8,128)(2,1)S(1)} %get-tuple-element.39), channel_id=1, source_target_pairs={{0,16},{8,24},{16,0},{24,8},{1,17},{9,25},{17,1},{25,9},{2,18},{10... | collective-permute-start | bytes 933896 | tf_op jit(solution)/shard_map/ppermute | solution.py:713
  22.3 31.1 %collective-permute-start = (bf16[2,304,256]{2,1,0:T(8,128)(2,1)S(1)}, bf16[2,304,256]{2,1,0:T(8,128)(2,1)S(1)}, u32[]{:S(2)}, u32[]{:S(2)}) collective-permute-start(bf16[2,304,256]{2,1,0:T(8,128)(2,1)S(1)} %get-tuple-element.40), channel_id=1, source_target_pairs={{0,8},{8,16},{16,24},{24,0},{1,9},{9,17},{17,25},{25,1},{2,10},{10... | collective-permute-start | bytes 933896 | tf_op jit(solution)/shard_map/ppermute | solution.py:713
  53.4 0.7 copy-start.1
  53.4 0.9 copy-start.2
  53.4 1.0 copy-start.3
  69.7 53.1 %copy-start = (f32[8,273,224]{2,1,0:T(8,128)S(1)}, f32[8,273,224]{2,1,0:T(8,128)}, u32[]{:S(2)}) copy-start(f32[8,273,224]{2,1,0:T(8,128)} %get-tuple-element.31) | copy-start | bytes 5870596
  122.8 2.1 %copy-start.4 = (bf16[64,1792]{1,0:T(8,128)(2,1)S(1)}, bf16[64,1792]{1,0:T(8,128)(2,1)}, u32[]{:S(2)}) copy-start(bf16[64,1792]{1,0:T(8,128)(2,1)} %get-tuple-element.46) | copy-start | bytes 688132

commit v2 on v1

--- a/solution.py
+++ b/solution.py
@@ -1,3 +1,4 @@
+import functools
 import math
 
 import jax
@@ -314,7 +315,7 @@
     return me, core, sib, (me, xn, yn, dg)
 
 
-def enter():
+def enter(groups):
     me = lax.axis_index("tok")
     barrier = pltpu.get_barrier_semaphore()
     for step in range(1, 8):
@@ -324,7 +325,14 @@
             device_id={"tok": (me + step) % 8},
             device_id_type=pl.DeviceIdType.MESH,
         )
-    pl.semaphore_wait(barrier, 7)
+    for step in range(1, groups):
+        pl.semaphore_signal(
+            barrier,
+            inc=1,
+            device_id={"group": (lax.axis_index("group") + step) % groups},
+            device_id_type=pl.DeviceIdType.MESH,
+        )
+    pl.semaphore_wait(barrier, 6 + groups)
 
 
 def remote(src, dst, send, recv, target):
@@ -342,82 +350,101 @@
     return ref.at[pl.ds(pl.multiple_of(index * rows, rows), rows)]
 
 
-def gather_rows(own_ref, all_ref, rows, send, recv):
+def gather_rows(own_ref, all_ref, rows, send, recv, work):
     me, core, sib, peers = places()
     home = block_at(all_ref, me, rows)
     out = []
-    for k in (3, 1, 2):
+    for k in (1, 2, 3):
         copy = remote(own_ref, home, send.at[k], recv.at[k], peers[k])
         copy.start()
         out.append(copy)
     copy = remote(own_ref, home, send.at[4], recv.at[4], sib)
     copy.start()
     out.append(copy)
-    for k in (1, 2, 3):
+    home[...] = own_ref[...]
+
+    def forward(k):
         landed = block_at(all_ref, peers[k], rows)
         remote(own_ref, landed, send.at[k], recv.at[k], peers[k]).wait_recv()
         copy = remote(landed, landed, send.at[4 + k], recv.at[4 + k], sib)
         copy.start()
         out.append(copy)
-    for k in range(4):
-        other = peers[k] + 1 - 2 * core
-        landed = block_at(all_ref, other, rows)
+
+    def from_sibling(k):
+        landed = block_at(all_ref, peers[k] + 1 - 2 * core, rows)
         remote(landed, landed, send.at[4 + k], recv.at[4 + k], sib).wait_recv()
+
+    from_sibling(0)
+    forward(1)
+    from_sibling(1)
+    work(me // 4)
+    forward(2)
+    forward(3)
+    from_sibling(2)
+    from_sibling(3)
+    work(1 - me // 4)
     for copy in out:
         copy.wait_send()
 
 
-def scatter_sum(part_ref, sib_ref, pair_ref, far_ref, rows, send, recv):
+def scatter_parts(part_ref, sib_ref, pair_ref, far_ref, rows, send, recv):
     me, core, sib, peers = places()
-    out = []
-    for k in (3, 1, 2, 0):
+    near, far = {}, {}
+
+    def emit(k):
         theirs = peers[k] + 1 - 2 * core
         copy = remote(block_at(part_ref, theirs, rows), sib_ref.at[k], send.at[k], recv.at[k], sib)
         copy.start()
-        out.append(copy)
-    for place, k in enumerate((3, 1, 2)):
-        out[place].wait_recv()
+        near[k] = copy
+
+    def flush(k):
+        near[k].wait_recv()
         pair_ref[k] = (
             block_at(part_ref, peers[k], rows)[...].astype(f32) + sib_ref[k].astype(f32)
         ).astype(bf16)
         copy = remote(pair_ref.at[k], far_ref.at[k], send.at[4 + k], recv.at[4 + k], peers[k])
         copy.start()
-        out.append(copy)
-    out[3].wait_recv()
-    total = block_at(part_ref, me, rows)[...].astype(f32) + sib_ref[0].astype(f32)
-    for place, k in enumerate((3, 1, 2)):
-        out[4 + place].wait_recv()
-    for k in (1, 2, 3):
-        total = total + far_ref[k].astype(f32)
-    for copy in out:
-        copy.wait_send()
-    return total
-
-
-def token_kernel(own_ref, all_ref, held, send, recv, local):
-    rows = own_ref.shape[0]
-    enter()
-    me = lax.axis_index("tok")
-    copy = pltpu.make_async_copy(own_ref, block_at(held, me, rows), local)
-    copy.start()
-    gather_rows(own_ref, held, rows, send, recv)
-    copy.wait()
-    all_ref[...] = held[...]
-
-
-def pick_kernel(slot_ref, state_ref, norm_ref, conv_ref, out_ref):
-    phi_size, columns = state_ref.shape[1], state_ref.shape[2]
-    head_count = norm_ref.shape[2]
-    heads = slot_ref[8]
+        far[k] = copy
+
+    def finish():
+        near[0].wait_recv()
+        total = block_at(part_ref, me, rows)[...].astype(f32) + sib_ref[0].astype(f32)
+        for k in (1, 2, 3):
+            far[k].wait_recv()
+            total = total + far_ref[k].astype(f32)
+        for k in (0, 1, 2, 3):
+            near[k].wait_send()
+        for k in (1, 2, 3):
+            far[k].wait_send()
+        return total
+
+    return emit, flush, finish
+
+
+def pick_kernel(slot_ref, state_hbm, norm_ref, conv_ref, out_ref, held, load):
+    phi_size, columns = state_hbm.shape[0], state_hbm.shape[2]
+    head_count = norm_ref.shape[1]
+    copies = []
+    for i in range(8):
+        copy = pltpu.make_async_copy(state_hbm.at[:, slot_ref[i], :], held.at[i], load.at[i])
+        copy.start()
+        copies.append(copy)
+    first_head = slot_ref[8]
     row = lax.broadcasted_iota(jnp.int32, (head_count, wide), 0)
     col = lax.broadcasted_iota(jnp.int32, (head_count, wide), 1)
-    choose = ((col >= columns) & (col < columns + 2) & (row == heads + col - columns)).astype(f32)
-    out_ref[0] = jnp.zeros((slot_rows, wide), bf16)
-    out_ref[0, 0:phi_size, :] = dot_nn(
-        norm_ref[0].astype(bf16), choose.astype(bf16)
+    choose = (
+        (col >= columns) & (col < columns + 2) & (row == first_head + col - columns)
     ).astype(bf16)
-    out_ref[0, 0:phi_size, 0:columns] = state_ref[0].astype(bf16)
-    out_ref[0, feat_rows : feat_rows + 2, 0:columns] = conv_ref[0]
+    for i in range(8):
+        slot = slot_ref[i]
+        norms = lax.dot_general(
+            norm_ref[slot].astype(bf16), choose, (((0,), (0,)), ((), ())), preferred_element_type=f32
+        )
+        out_ref[i, phi_size - 1 : slot_rows, :] = jnp.zeros((slot_rows - phi_size + 1, wide), bf16)
+        out_ref[i, 0:phi_size, :] = norms.astype(bf16)
+        out_ref[i, feat_rows : feat_rows + 2, 0:columns] = conv_ref[slot]
+        copies[i].wait()
+        out_ref[i, 0:phi_size, 0:columns] = held[i].astype(bf16)
 
 
 def head_zero(shape, columns):
@@ -426,16 +453,56 @@
 
 
 def local_kernel(
-    info_ref, rows_ref, gain_ref, mixer_ref, qk_ref, qk_out, v_out, conv_out, gate_out, acc_out, normed
+    groups,
+    info_ref,
+    own_ref,
+    packed_ref,
+    gain_ref,
+    mixer_ref,
+    qk_hbm,
+    qk_out,
+    v_out,
+    conv_out,
+    gate_out,
+    acc_out,
+    slots_out,
+    rows_ref,
+    normed,
+    qk_ref,
+    landed,
+    send,
+    recv,
+    send_z,
+    recv_z,
+    load,
 ):
+    rows = own_ref.shape[0]
     all_rows = rows_ref.shape[0]
     columns = mixer_ref.shape[1]
     feature = 16
-    half = 256
-
-    @pl.loop(0, all_rows // half)
-    def _(step):
-        span = pl.ds(pl.multiple_of(step * half, half), half)
+    half = all_rows // 2
+    me = lax.axis_index("tok")
+    group_now = lax.axis_index("group")
+    picked = pl.ds(pl.multiple_of(me * 2 * feature, 2 * feature), 2 * feature)
+    qk_copy = pltpu.make_async_copy(qk_hbm.at[:, picked, :], qk_ref, load)
+    qk_copy.start()
+    enter(groups)
+    shifts = []
+    for step in range(1, groups):
+        copy = pltpu.make_async_remote_copy(
+            src_ref=packed_ref.at[pl.ds(2 * step, 2)],
+            dst_ref=landed.at[step - 1],
+            send_sem=send_z.at[step - 1],
+            recv_sem=recv_z.at[step - 1],
+            device_id={"group": (group_now + step) % groups},
+            device_id_type=pl.DeviceIdType.MESH,
+        )
+        copy.start()
+        shifts.append(copy)
+    qk_copy.wait()
+
+    def project(which):
+        span = pl.ds(pl.multiple_of(which * half, half), half)
         x = rows_ref[span, :].astype(f32)
         scale = lax.rsqrt(jnp.mean(x * x, axis=-1, keepdims=True) + epsilon)
         normed[...] = (x * scale * gain_ref[0:1, :]).astype(bf16)
@@ -444,6 +511,8 @@
         conv_out[span, :] = dot_nt(normed[...], mixer_ref[1])
         gate_out[span, :] = dot_nt(normed[...], mixer_ref[2])
         qk_out[span, :] = dot_nt(normed[...], qk_ref[...].reshape(4 * feature, qk_ref.shape[2]))
+
+    gather_rows(own_ref, rows_ref, rows, send, recv, project)
 
     block = 128
 
@@ -467,6 +536,11 @@
             found.append(dot_nn(w, v_out[...]))
         acc_out[span, :] = jnp.where(head_zero((block, wide), columns), found[0], found[1])
 
+    slots_out[0:2] = packed_ref[0:2]
+    for step in range(1, groups):
+        shifts[step - 1].wait()
+        slots_out[2 * step : 2 * step + 2] = landed[step - 1]
+
 
 def carried_kernel(
     info_ref,
@@ -475,10 +549,7 @@
     conv_ref,
     gate_ref,
     acc_ref,
-    slots_a,
-    slots_b,
-    slots_c,
-    slots_d,
+    slots_ref,
     first_ref,
     second_ref,
     add_ref,
@@ -486,9 +557,9 @@
     second_t_ref,
     add_t_ref,
     taps_ref,
-    weight_ref,
-    mixed_out,
-    state_out,
+    att_out,
+    gated_out,
+    state_hbm,
     norm_out,
     cache_out,
     num,
@@ -497,10 +568,16 @@
     prev_two,
     phi_q,
     phi_k,
-    att,
+    fresh_ref,
+    store,
 ):
     all_rows, columns = conv_ref.shape
-    phi_size = state_out.shape[1]
+    phi_size = state_hbm.shape[0]
+    norms = jnp.zeros((16, feat_rows), f32)
+    norm_row = lax.broadcasted_iota(jnp.int32, (16, 128), 0)
+    norm_col = lax.broadcasted_iota(jnp.int32, (16, 128), 1) - (columns - 128)
+    pair = lax.broadcasted_iota(jnp.int32, (2, columns), 0)
+    copies = []
     hi = qk_ref[...].astype(bf16)
     lo = (qk_ref[...] - hi.astype(f32)).astype(bf16)
     for h in range(2):
@@ -519,23 +596,28 @@
     row_zero = head_zero((all_rows, wide), columns)
     state_zero = head_zero((feat_rows, wide), columns)
     for index in range(8):
-        slots = (slots_a, slots_b, slots_c, slots_d)[index // 2]
         request = info_ref[24 + index]
         begin = info_ref[request]
         length = info_ref[8 + request]
         cached = info_ref[16 + request]
         end = begin + length
         live = jnp.where(cached > 0, 1.0, 0.0).astype(f32)
-        state = slots[index % 2, 0:feat_rows, :]
+        state = slots_ref[index, 0:feat_rows, :]
         member = (i >= begin) & (i < end)
         carried = jnp.where(row_zero, dot_nn(phi_q[0], state), dot_nn(phi_q[1], state)) * live
         num[...] += jnp.where(member, carried, 0.0)
         mine = jnp.where(member, v_ref[...].astype(f32), 0.0).astype(bf16)
         added = jnp.where(state_zero, dot_nn(phi_k[0], mine), dot_nn(phi_k[1], mine))
         fresh = state.astype(f32) * live + added
-        state_out[request] = fresh[0:phi_size, 0:columns]
-        norm_out[request] = fresh[0:feat_rows, 128:256]
-        tail = slots[index % 2, feat_rows:slot_rows, 0:columns].astype(f32)
+        fresh_ref[index] = fresh[0:phi_size, 0:columns]
+        copy = pltpu.make_async_copy(
+            fresh_ref.at[index], state_hbm.at[:, request, :], store.at[index]
+        )
+        copy.start()
+        copies.append(copy)
+        choose = ((norm_row % 8 == request) & (norm_row // 8 == norm_col)).astype(bf16)
+        norms = norms + dot_nt(choose, fresh[:, 128:256].astype(bf16))
+        tail = slots_ref[index, feat_rows:slot_rows, 0:columns].astype(f32)
         newest = tail[1:2] * live
         oldest = tail[0:1] * jnp.where(cached >= 2, 1.0, 0.0).astype(f32)
         prev_one[...] = jnp.where(i == begin, newest, prev_one[...])
@@ -544,28 +626,25 @@
         )
         final = shifted[pl.ds(7 + end, 1), :]
         before = shifted[pl.ds(6 + end, 1), :]
-        cache_out[request, 0:1, :] = jnp.where(length >= 2, before, newest)
-        cache_out[request, 1:2, :] = final
+        before = jnp.where(length >= 2, before, newest)
+        cache_out[request] = jnp.where(pair == 0, before, final).astype(bf16)
     col = lax.broadcasted_iota(jnp.int32, (all_rows, wide), 1)
     den = jnp.where(col < columns // 2, num[:, columns : columns + 1], num[:, columns + 1 : columns + 2])
-    att[...] = (num[...] / den).astype(bf16)
+    att_out[...] = (num[...] / den).astype(bf16)
     convolved = (
         taps_ref[0:1] * conv_ref[...] + taps_ref[1:2] * prev_one[...] + taps_ref[2:3] * prev_two[...]
     )
-    gated = (convolved * gate_ref[...]).astype(bf16)
-    prev_one[...] = gated.astype(f32)
-
-    @pl.loop(0, all_rows // 256)
-    def _(step):
-        span = pl.ds(pl.multiple_of(step * 256, 256), 256)
-        mixed_out[span, :] = (
-            dot_nn(att[span, 0:columns], weight_ref[0])
-            + dot_nn(prev_one[span, :].astype(bf16), weight_ref[1])
-        ).astype(bf16)
+    gated_out[...] = (convolved * gate_ref[...]).astype(bf16)
+    norm_out[...] = jnp.zeros(norm_out.shape, bf16)
+    norm_out[:, 0:feat_rows] = norms.astype(bf16)
+    for copy in copies:
+        copy.wait()
 
 
 def ffn_kernel(
-    part_ref,
+    att_ref,
+    gated_ref,
+    weight_ref,
     own_ref,
     gain_ref,
     norm_ref,
@@ -583,6 +662,7 @@
     far_b,
     own_normed,
     normed,
+    part_one,
     part_two,
     norms,
     send_a,
@@ -596,21 +676,32 @@
     load,
 ):
     rows = own_ref.shape[0]
-    all_rows = part_ref.shape[0]
+    half = att_ref.shape[0] // 2
+    columns = weight_ref.shape[1]
     up_copy = pltpu.make_async_copy(up_hbm, up, load.at[0])
     down_copy = pltpu.make_async_copy(down_hbm, down, load.at[1])
     up_copy.start()
     down_copy.start()
-    enter()
+    enter(1)
     me = lax.axis_index("tok")
+
+    def project(which):
+        span = pl.ds(pl.multiple_of(which * half, half), half)
+        part_one[span, :] = (
+            dot_nn(att_ref[span, 0:columns], weight_ref[0])
+            + dot_nn(gated_ref[span, :], weight_ref[1])
+        ).astype(bf16)
+
+    emit, flush, finish = scatter_parts(part_one, sib_a, pair_a, far_a, rows, send_a, recv_a)
+    project(1 - me // 4)
+    emit(3)
+    emit(2)
+    project(me // 4)
+    emit(1)
+    emit(0)
+    for k in (3, 2, 1):
+        flush(k)
     small = []
-    total = scatter_sum(part_ref, sib_a, pair_a, far_a, rows, send_a, recv_a)
-    residual = own_ref[...].astype(f32) + total
-    scale = lax.rsqrt(jnp.mean(residual * residual, axis=-1, keepdims=True) + epsilon)
-    own_normed[...] = (residual * scale * gain_ref[1:2, :]).astype(bf16)
-    mine = pltpu.make_async_copy(own_normed, block_at(normed, me, rows), load.at[2])
-    mine.start()
-    gather_rows(own_normed, normed, rows, send_g, recv_g)
     for step in range(1, 8):
         copy = remote(
             norm_ref, norms.at[me], send_n.at[step - 1], recv_n.at[step - 1], (me + step) % 8
@@ -618,21 +709,32 @@
         copy.start()
         small.append(copy)
     norms[me] = norm_ref[...]
-    mine.wait()
+    residual = own_ref[...].astype(f32) + finish()
+    scale = lax.rsqrt(jnp.mean(residual * residual, axis=-1, keepdims=True) + epsilon)
+    own_normed[...] = (residual * scale * gain_ref[1:2, :]).astype(bf16)
     up_copy.wait()
     down_copy.wait()
-    half = 256
-
-    @pl.loop(0, all_rows // half)
-    def _(step):
-        span = pl.ds(pl.multiple_of(step * half, half), half)
+    emit, flush, finish = scatter_parts(part_two, sib_b, pair_b, far_b, rows, send_b, recv_b)
+
+    def feed(which):
+        span = pl.ds(pl.multiple_of(which * half, half), half)
         gate = dot_nt(normed[span, :], up[0])
         lift = dot_nt(normed[span, :], up[1])
         hidden = (gate / (1.0 + jnp.exp(-gate)) * lift).astype(bf16)
         part_two[span, :] = dot_nn(hidden, down[...]).astype(bf16)
 
-    total = scatter_sum(part_two, sib_b, pair_b, far_b, rows, send_b, recv_b)
-    out_ref[...] = (residual + total).astype(bf16)
+    done = []
+
+    def feed_and_send(which):
+        feed(which)
+        for k in (3, 2) if done else (1, 0):
+            emit(k)
+        for k in (3, 2) if done else (1,):
+            flush(k)
+        done.append(which)
+
+    gather_rows(own_normed, normed, rows, send_g, recv_g, feed_and_send)
+    out_ref[...] = (residual + finish()).astype(bf16)
     for step in range(1, 8):
         small[step - 1].wait_send()
         remote(
@@ -692,85 +794,62 @@
     info = jnp.concatenate([starts, lengths, cached_lengths, take]).astype(jnp.int32)
     picks = jnp.concatenate([give, (tok_now * heads)[None].astype(jnp.int32)])
 
+    in_any = pl.BlockSpec(memory_space=pl.ANY)
     packed = pl.pallas_call(
         pick_kernel,
-        grid_spec=pltpu.PrefetchScalarGridSpec(
-            num_scalar_prefetch=1,
-            grid=(2 * groups,),
-            in_specs=[
-                pl.BlockSpec((1, phi_size, columns), lambda i, s: (s[i], 0, 0)),
-                pl.BlockSpec((1, phi_size, head_count), lambda i, s: (s[i], 0, 0)),
-                pl.BlockSpec((1, 2, columns), lambda i, s: (s[i], 0, 0)),
-            ],
-            out_specs=pl.BlockSpec((1, slot_rows, wide), lambda i, s: (i, 0, 0)),
-        ),
+        in_specs=[in_smem, in_any, in_vmem, in_vmem],
+        out_specs=in_vmem,
         out_shape=shape((2 * groups, slot_rows, wide), bf16),
+        scratch_shapes=[VMEM((8, phi_size, columns), f32), dma((8,))],
+        compiler_params=pltpu.CompilerParams(vmem_limit_bytes=big_vmem),
         name="pick_slots",
-    )(picks, cached_states, cached_norms, conv_cache)
-    arrived = [packed[0:2]]
-    for step in range(1, groups):
-        ring = [(g, (g + step) % groups) for g in range(groups)]
-        arrived.append(lax.ppermute(packed[2 * step : 2 * step + 2], "group", ring))
-
-    whole_rows = pl.pallas_call(
-        token_kernel,
-        out_shape=shape((all_rows, width), bf16),
-        in_specs=[in_vmem],
-        out_specs=in_vmem,
-        scratch_shapes=[VMEM((all_rows, width), bf16), dma((8,)), dma((8,)), dma],
-        compiler_params=pltpu.CompilerParams(
-            collective_id=0, has_side_effects=True, vmem_limit_bytes=big_vmem
-        ),
-        cost_estimate=pl.CostEstimate(flops=0, bytes_accessed=30000000, transcendentals=0),
-        name="gather_tokens",
-    )(tokens)
-
-    def full(*dims):
-        return pl.BlockSpec(dims, lambda i, s: (0,) * len(dims))
-
-    tok_pick = jnp.concatenate([info, tok_now[None].astype(jnp.int32)])
-    qk, vext, conv_in, gate, acc = pl.pallas_call(
-        local_kernel,
-        grid_spec=pltpu.PrefetchScalarGridSpec(
-            num_scalar_prefetch=1,
-            grid=(1,),
-            in_specs=[
-                full(all_rows, width),
-                full(2, width),
-                full(3, columns, width),
-                pl.BlockSpec((2, heads * feature, width), lambda i, s: (0, s[32], 0)),
-            ],
-            out_specs=[
-                full(all_rows, 4 * feature),
-                full(all_rows, wide),
-                full(all_rows, columns),
-                full(all_rows, columns),
-                full(all_rows, wide),
-            ],
-            scratch_shapes=[VMEM((256, width), bf16)],
-        ),
+    )(
+        picks,
+        jnp.transpose(cached_states, (1, 0, 2)),
+        jnp.transpose(cached_norms, (0, 2, 1)),
+        conv_cache,
+    )
+
+    qk, vext, conv_in, gate, acc, slots = pl.pallas_call(
+        functools.partial(local_kernel, groups),
+        in_specs=[in_smem, in_vmem, in_vmem, in_vmem, in_vmem, in_any],
+        out_specs=[in_vmem] * 6,
         out_shape=[
             shape((all_rows, 4 * feature), f32),
             shape((all_rows, wide), bf16),
             shape((all_rows, columns), f32),
             shape((all_rows, columns), f32),
             shape((all_rows, wide), f32),
+            shape((2 * groups, slot_rows, wide), bf16),
         ],
-        compiler_params=pltpu.CompilerParams(vmem_limit_bytes=big_vmem),
-        cost_estimate=pl.CostEstimate(flops=2000000000, bytes_accessed=30000000, transcendentals=0),
-        name="local_attention",
-    )(tok_pick, whole_rows, norm_gains, mixer_weight, qk_weight)
+        scratch_shapes=[
+            VMEM((all_rows, width), bf16),
+            VMEM((all_rows // 2, width), bf16),
+            VMEM((2, heads * feature, width), bf16),
+            VMEM((groups - 1, 2, slot_rows, wide), bf16),
+            dma((8,)),
+            dma((8,)),
+            dma((groups - 1,)),
+            dma((groups - 1,)),
+            dma,
+        ],
+        compiler_params=pltpu.CompilerParams(
+            collective_id=0, has_side_effects=True, vmem_limit_bytes=big_vmem
+        ),
+        name="gather_and_local_attention",
+    )(info, tokens, packed, norm_gains, mixer_weight, qk_weight)
 
     first, second, add = feature_tables(heads, feature)
-    mixed, new_states, norm_wide, cache_next = pl.pallas_call(
+    att, gated, new_states, share, cache_next = pl.pallas_call(
         carried_kernel,
-        in_specs=[in_smem] + [in_vmem] * 17,
-        out_specs=[in_vmem] * 4,
+        in_specs=[in_smem] + [in_vmem] * 13,
+        out_specs=[in_vmem, in_vmem, in_any, in_vmem, in_vmem],
         out_shape=[
-            shape((all_rows, width), bf16),
-            shape((requests, phi_size, columns), f32),
-            shape((requests, feat_rows, 128), f32),
-            shape((requests, 2, columns), f32),
+            shape((all_rows, wide), bf16),
+            shape((all_rows, columns), bf16),
+            shape((phi_size, requests, columns), f32),
+            shape((heads * requests, 384), bf16),
+            shape((requests, 2, columns), bf16),
         ],
         scratch_shapes=[
             VMEM((all_rows, wide), f32),
@@ -779,7 +858,8 @@
             VMEM((all_rows, columns), f32),
             VMEM((2, all_rows, feat_rows), bf16),
             VMEM((2, feat_rows, all_rows), bf16),
-            VMEM((all_rows, wide), bf16),
+            VMEM((8, phi_size, columns), f32),
+            dma((8,)),
         ],
         compiler_params=pltpu.CompilerParams(vmem_limit_bytes=big_vmem),
         name="carried_states",
@@ -790,7 +870,7 @@
         conv_in,
         gate,
         acc,
-        *arrived,
+        slots,
         jnp.asarray(first[:heads], bf16),
         jnp.asarray(second[:heads], bf16),
         jnp.asarray(add, f32),
@@ -798,19 +878,12 @@
         jnp.asarray(second[heads:].transpose(0, 2, 1), bf16),
         jnp.asarray(add.T, f32),
         conv_weight,
-        out_weight,
-    )
-    low = columns - 128
-    share = norm_wide[:, :, low : low + heads].astype(bf16)
-    share = jnp.transpose(share, (2, 0, 1)).reshape(heads * requests, feat_rows)
-    share = jnp.pad(share, ((0, 0), (0, 384 - feat_rows)))
-
+    )
     units = ffn_weight.shape[1]
     blocks = VMEM((4, rows, width), bf16)
-    in_any = pl.BlockSpec(memory_space=pl.ANY)
     layer_out, norms = pl.pallas_call(
         ffn_kernel,
-        in_specs=[in_vmem, in_vmem, in_vmem, in_vmem, in_any, in_any],
+        in_specs=[in_vmem] * 6 + [in_any, in_any],
         out_specs=[in_vmem, in_vmem],
         out_shape=[shape((rows, width), bf16), shape((8,) + share.shape, bf16)],
         scratch_shapes=[
@@ -825,6 +898,7 @@
             VMEM((rows, width), bf16),
             VMEM((all_rows, width), bf16),
             VMEM((all_rows, width), bf16),
+            VMEM((all_rows, width), bf16),
             VMEM((8,) + share.shape, bf16),
         ]
         + [dma((8,))] * 8
@@ -833,10 +907,10 @@
             collective_id=1, has_side_effects=True, vmem_limit_bytes=big_vmem
         ),
         name="sum_and_ffn",
-    )(mixed, tokens, norm_gains, share, ffn_weight, down_weight)
+    )(att, gated, out_weight, tokens, norm_gains, share, ffn_weight, down_weight)
     norms = norms.reshape(8, heads, requests, -1)[:, :, :, :phi_size].astype(f32)
     new_norms = jnp.transpose(norms, (2, 3, 0, 1)).reshape(requests, phi_size, head_count)
-    return (layer_out, new_states, new_norms, cache_next.astype(bf16))
+    return (layer_out, jnp.transpose(new_states, (1, 0, 2)), new_norms, cache_next)
 
 
 def device_function(mesh):

time: 127 us -> 111 us (0.87)
  local copies, waits for them, and re-layouts: 17.1 us -> 3.87 us
  starting transfers between devices: 5.57 us -> 0 us
  Pallas kernels: 96.8 us -> 100 us
    unnamed x19 -> x2, local copies, waits for them, and re-layouts: 10.3 us -> 2.15 us
    ppermute x3 -> x0, starting transfers between devices: 5.57 us -> none  [fast_device(): arrived.append(lax.ppermute(packed[2 * step:2 * step + 2], 'group', ring))]
    pallas_call x5 -> x4, Pallas kernels: 96.8 us -> 100 us  [the longest x1 48.4 us: fast_device(): pl.pallas_call(ffn_kernel, in_specs=[in_vmem] * 6 + [in_any, in_any], out...]
    slice x1 -> x0, local copies, waits for them, and re-layouts: 2.08 us -> none  [fast_device(): arrived.append(lax.ppermute(packed[2 * step:2 * step + 2], 'group', ring))]
    transpose x2 -> x0, local copies, waits for them, and re-layouts: 1.79 us -> none  [fast_device(): share = jnp.transpose(share, (2, 0, 1)).reshape(heads * requests, feat_rows)]
    convert_element_type x1 -> x0, other arithmetic: 1.32 us -> none  [fast_device(): return (layer_out, new_states, new_norms, cache_next.astype(bf16))]
  transfers between devices with their start and end apart: 3 -> 0, of which waited for: 0 -> 0; matrix products, arithmetic and copies ran while one was open for 1% -> 0% of each run, Pallas kernels for 21% -> 0%
where the time goes in v2:
time: 111 us
  Pallas kernels  100 us (90%)
  other arithmetic  5.95 us (5%)
  local copies, waits for them, and re-layouts  3.87 us (3%)
    pallas_call x1, Pallas kernels, fast_device(): pl.pallas_call(ffn_kernel, in_specs=[in_vmem] * 6 + [in_any, in_any], out...  48.4 us
    pallas_call x1, Pallas kernels, fast_device(): pl.pallas_call(functools.partial(local_kernel, groups), in_specs=[in_smem...  35.9 us
    pallas_call x1, Pallas kernels, fast_device(): pl.pallas_call(carried_kernel, in_specs=[in_smem] + [in_vmem] * 13, out_s...  11 us
    pallas_call x1, Pallas kernels, fast_device(): pl.pallas_call(pick_kernel, in_specs=[in_smem, in_any, in_vmem, in_vmem],...  4.88 us

profile of v2, /device:TPU:8, one launch (start us, length us, event | category | flops | bytes accessed | tf_op | source)
XLA Modules:
  0.0 110.7 jit_solution(3021782714201320568)
XLA Ops:
  0.7 0.5 broadcast.102
  1.2 1.3 %reduce.3 = s32[32]{0:T(128)S(1)} reduce(s32[32,1]{0,1:T(1,128)} %param.33, s32[]{:T(128)} %broadcast.102), dimensions={1}, to_apply=%param.33.reduce_sub_computation.3 | reduce | bytes 260 | tf_op args[13]
  2.5 0.8 reduce-window.9
  3.3 0.7 bitcast_subtract_fusion
  4.0 0.1 reshape_squeeze.3
  4.1 0.2 fusion
  4.3 0.1 copy.27
  4.4 0.1 reshape.116
  4.5 1.3 %pad_add_fusion.2.info_ref = s32[32]{0:T(128)} fusion(s32[8]{0:T(128)S(1)} %reshape.116, s32[8]{0:T(128)} %param.31, s32[8]{0:T(128)} %bitcast.31, s32[8]{0:T(128)S(1)} %bitcast_subtract_fusion), kind=kLoop, calls=%fused_computation.22 | loop fusion | flops 96 | bytes 256 | tf_op jit(solution)/shard_map/concatenate | solution.py:794
  5.7 0.6 gather_fusion
  6.3 0.2 select_reduce_fusion.1
  6.5 0.1 copy.28
  6.5 0.1 reshape.117
  6.6 0.6 pad_add_fusion.3.slot_ref
  7.2 4.9 %pick_slots.1.packed_ref = bf16[8,304,256]{2,1,0:T(8,128)(2,1)} custom-call(s32[9]{0:T(128)} %pad_add_fusion.3.slot_ref, f32[273,8,224]{2,1,0:T(8,128)} %bitcast.22, f32[8,16,273]{2,1,0:T(8,128)} %bitcast.24, bf16[8,2,224]{2,1,0:T(2,128)(2,1)} %conv_ref.1), custom_call_target="tpu_custom_call" | custom-call | tf_op jit(solution)/shard_map/pick_slots/pallas_call | solution.py:798
  12.1 35.9 %gather_and_local_attention.1 = (f32[512,64]{1,0:T(8,128)}, bf16[512,256]{1,0:T(8,128)(2,1)}, f32[512,224]{1,0:T(8,128)}, f32[512,224]{1,0:T(8,128)}, f32[512,256]{1,0:T(8,128)}, /*index=5*/bf16[8,304,256]{2,1,0:T(8,128)(2,1)}) custom-call(s32[32]{0:T(128)} %pad_add_fusion.2.info_ref, bf16[64,1792]{1,0:T(8,128)(2,1)} %own_ref.3, ...), custom_call_target="tpu_custom_call" | custom-call | tf_op jit(solution)/shard_map/gather_and_local_attention/pallas_call | solution.py:813
  48.0 11.0 %carried_states.1 = (bf16[512,256]{1,0:T(8,128)(2,1)}, bf16[512,224]{1,0:T(8,128)(2,1)}, f32[273,8,224]{2,1,0:T(8,128)}, bf16[16,384]{1,0:T(8,128)(2,1)}, bf16[8,2,224]{2,1,0:T(2,128)(2,1)}) custom-call(s32[32]{0:T(128)} %pad_add_fusion.2.info_ref, f32[512,64]{1,0:T(8,128)} %get-tuple-element.17.qk_ref, bf16[512,256]{1,0:T(8,128)(2,1)} %get-tuple-element.18.v_ref, ...), custom_call_target="tpu_custom_call" | custom-call | tf_op jit(solution)/shard_map/carried_states/pallas_call | solution.py:843
  59.0 48.4 %sum_and_ffn.1 = (bf16[64,1792]{1,0:T(8,128)(2,1)}, bf16[8,16,384]{2,1,0:T(8,128)(2,1)}) custom-call(bf16[512,256]{1,0:T(8,128)(2,1)} %get-tuple-element.23.att_ref, bf16[512,224]{1,0:T(8,128)(2,1)} %get-tuple-element.24.gated_ref, bf16[2,224,1792]{2,1,0:T(8,128)(2,1)} %weight_ref.1, bf16[64,1792]{1,0:T(8,128)(2,1)} %own_ref.3, f32[2,1792]{1,0:T(2,128)} %gain_ref.3, ...), custom_call_target="tpu_custom_call" | custom-call | tf_op jit(solution)/shard_map/sum_and_ffn/pallas_call | solution.py:884
  107.5 0.9 slice_convert_fusion
  108.4 0.7 copy.30
  109.1 1.6 %copy.32 = bf16[64,1792]{1,0:T(8,128)(2,1)} copy(bf16[64,1792]{1,0:T(8,128)(2,1)} %get-tuple-element.38) | data formatting | bytes 458752
  (6 shorter events, 0.1 us)

commit v3 on v2

--- a/solution.py
+++ b/solution.py
@@ -374,11 +374,11 @@
         landed = block_at(all_ref, peers[k] + 1 - 2 * core, rows)
         remote(landed, landed, send.at[4 + k], recv.at[4 + k], sib).wait_recv()
 
+    forward(1)
+    forward(2)
     from_sibling(0)
-    forward(1)
     from_sibling(1)
     work(me // 4)
-    forward(2)
     forward(3)
     from_sibling(2)
     from_sibling(3)
@@ -421,22 +421,34 @@
     return emit, flush, finish
 
 
-def pick_kernel(slot_ref, state_hbm, norm_ref, conv_ref, out_ref, held, load):
+def two_requests(source_ref, row_group, named):
+    first, last = jnp.int32(7), jnp.int32(0)
+    for r in range(8):
+        last = jnp.where(source_ref[row_group * 8 + r] == named, r, last)
+        first = jnp.where(source_ref[row_group * 8 + 7 - r] == named, 7 - r, first)
+    return [first, last]
+
+
+def pick_kernel(groups, source_ref, state_hbm, norm_ref, conv_ref, out_ref, held, load):
     phi_size, columns = state_hbm.shape[0], state_hbm.shape[2]
     head_count = norm_ref.shape[1]
+    group_now = lax.axis_index("group")
+    wanted = []
+    for step in range(groups):
+        wanted += two_requests(source_ref, (group_now + step) % groups, group_now)
     copies = []
     for i in range(8):
-        copy = pltpu.make_async_copy(state_hbm.at[:, slot_ref[i], :], held.at[i], load.at[i])
+        copy = pltpu.make_async_copy(state_hbm.at[:, wanted[i], :], held.at[i], load.at[i])
         copy.start()
         copies.append(copy)
-    first_head = slot_ref[8]
+    first_head = lax.axis_index("tok") * 2
     row = lax.broadcasted_iota(jnp.int32, (head_count, wide), 0)
     col = lax.broadcasted_iota(jnp.int32, (head_count, wide), 1)
     choose = (
         (col >= columns) & (col < columns + 2) & (row == first_head + col - columns)
     ).astype(bf16)
     for i in range(8):
-        slot = slot_ref[i]
+        slot = wanted[i]
         norms = lax.dot_general(
             norm_ref[slot].astype(bf16), choose, (((0,), (0,)), ((), ())), preferred_element_type=f32
         )
@@ -523,8 +535,10 @@
         query = qk_out[span, :]
         i = lax.broadcasted_iota(jnp.int32, (block, 1), 0) + low
         begin = jnp.zeros((block, 1), jnp.int32)
+        start = jnp.int32(0)
         for r in range(8):
-            begin = jnp.where(i >= info_ref[r], info_ref[r], begin)
+            begin = jnp.where(i >= start, start, begin)
+            start = start + info_ref[0, r]
         j = lax.broadcasted_iota(jnp.int32, (block, all_rows), 1)
         allowed = (j <= i) & (j >= begin)
         found = []
@@ -543,7 +557,10 @@
 
 
 def carried_kernel(
-    info_ref,
+    groups,
+    source_ref,
+    lengths_ref,
+    cached_ref,
     qk_ref,
     v_ref,
     conv_ref,
@@ -595,11 +612,17 @@
     i = lax.broadcasted_iota(jnp.int32, (all_rows, 1), 0)
     row_zero = head_zero((all_rows, wide), columns)
     state_zero = head_zero((feat_rows, wide), columns)
+    group_now = lax.axis_index("group")
+    taken = []
+    for step in range(groups):
+        taken += two_requests(source_ref, group_now, (group_now + groups - step) % groups)
     for index in range(8):
-        request = info_ref[24 + index]
-        begin = info_ref[request]
-        length = info_ref[8 + request]
-        cached = info_ref[16 + request]
+        request = taken[index]
+        begin = jnp.int32(0)
+        for r in range(7):
+            begin = begin + jnp.where(r < request, lengths_ref[0, r], 0)
+        length = lengths_ref[0, request]
+        cached = cached_ref[request]
         end = begin + length
         live = jnp.where(cached > 0, 1.0, 0.0).astype(f32)
         state = slots_ref[index, 0:feat_rows, :]
@@ -696,11 +719,12 @@
     project(1 - me // 4)
     emit(3)
     emit(2)
+    flush(3)
+    flush(2)
     project(me // 4)
     emit(1)
     emit(0)
-    for k in (3, 2, 1):
-        flush(k)
+    flush(1)
     small = []
     for step in range(1, 8):
         copy = remote(
@@ -726,11 +750,14 @@
     done = []
 
     def feed_and_send(which):
+        if done:
+            flush(1)
         feed(which)
         for k in (3, 2) if done else (1, 0):
             emit(k)
-        for k in (3, 2) if done else (1,):
-            flush(k)
+        if done:
+            flush(3)
+            flush(2)
         done.append(which)
 
     gather_rows(own_normed, normed, rows, send_g, recv_g, feed_and_send)
@@ -770,33 +797,15 @@
     feature = qk_weight.shape[1] // head_count
     heads = 2
     groups = lax.axis_size("group")
-    group_now = lax.axis_index("group")
-    tok_now = lax.axis_index("tok")
     shape = jax.ShapeDtypeStruct
     dma = pltpu.SemaphoreType.DMA
     in_vmem = pl.BlockSpec(memory_space=VMEM)
     in_smem = pl.BlockSpec(memory_space=pltpu.SMEM)
 
-    sources = state_source[:, 0].reshape(groups, requests)
-    request = jnp.arange(requests, dtype=jnp.int32)
-    shift = jnp.arange(groups, dtype=jnp.int32)
-
-    def ends_of(match):
-        low = jnp.min(jnp.where(match, request[None], requests - 1), axis=1)
-        high = jnp.max(jnp.where(match, request[None], 0), axis=1)
-        return jnp.stack([low, high], axis=1).reshape(-1).astype(jnp.int32)
-
-    give = ends_of(sources[(group_now + shift) % groups] == group_now)
-    own_sources = lax.dynamic_index_in_dim(sources, group_now, 0, keepdims=False)
-    take = ends_of(own_sources[None] == ((group_now + groups - shift) % groups)[:, None])
-    lengths = new_lengths[0]
-    starts = jnp.cumsum(lengths) - lengths
-    info = jnp.concatenate([starts, lengths, cached_lengths, take]).astype(jnp.int32)
-    picks = jnp.concatenate([give, (tok_now * heads)[None].astype(jnp.int32)])
-
+    sources = state_source.reshape(-1)
     in_any = pl.BlockSpec(memory_space=pl.ANY)
     packed = pl.pallas_call(
-        pick_kernel,
+        functools.partial(pick_kernel, groups),
         in_specs=[in_smem, in_any, in_vmem, in_vmem],
         out_specs=in_vmem,
         out_shape=shape((2 * groups, slot_rows, wide), bf16),
@@ -804,7 +813,7 @@
         compiler_params=pltpu.CompilerParams(vmem_limit_bytes=big_vmem),
         name="pick_slots",
     )(
-        picks,
+        sources,
         jnp.transpose(cached_states, (1, 0, 2)),
         jnp.transpose(cached_norms, (0, 2, 1)),
         conv_cache,
@@ -837,12 +846,12 @@
             collective_id=0, has_side_effects=True, vmem_limit_bytes=big_vmem
         ),
         name="gather_and_local_attention",
-    )(info, tokens, packed, norm_gains, mixer_weight, qk_weight)
+    )(new_lengths, tokens, packed, norm_gains, mixer_weight, qk_weight)
 
     first, second, add = feature_tables(heads, feature)
     att, gated, new_states, share, cache_next = pl.pallas_call(
-        carried_kernel,
-        in_specs=[in_smem] + [in_vmem] * 13,
+        functools.partial(carried_kernel, groups),
+        in_specs=[in_smem] * 3 + [in_vmem] * 13,
         out_specs=[in_vmem, in_vmem, in_any, in_vmem, in_vmem],
         out_shape=[
             shape((all_rows, wide), bf16),
@@ -864,7 +873,9 @@
         compiler_params=pltpu.CompilerParams(vmem_limit_bytes=big_vmem),
         name="carried_states",
     )(
-        info,
+        sources,
+        new_lengths,
+        cached_lengths,
         qk,
         vext,
         conv_in,

time: 111 us -> 105 us (0.946)
  other arithmetic: 5.95 us -> 0.91 us
  local copies, waits for them, and re-layouts: 3.87 us -> 2.35 us
    concatenate x2 -> x0, other arithmetic: 1.85 us -> none  [the longest x1 1.26 us: fast_device(): jnp.concatenate([starts, lengths, cached_lengths, take]).astype(jnp.int32)]
    unnamed x1 -> x0, other arithmetic: 1.32 us -> none
where the time goes in v3:
time: 105 us; the launch traced here: 104 us
  Pallas kernels  100 us (95%)
  local copies, waits for them, and re-layouts  2.35 us (2%)
    pallas_call x1, Pallas kernels, fast_device(): pl.pallas_call(ffn_kernel, in_specs=[in_vmem] * 6 + [in_any, in_any], out...  48.2 us
    pallas_call x1, Pallas kernels, fast_device(): pl.pallas_call(functools.partial(local_kernel, groups), in_specs=[in_smem...  35.9 us
    pallas_call x1, Pallas kernels, fast_device(): pl.pallas_call(functools.partial(carried_kernel, groups), in_specs=[in_sm...  11.1 us
    pallas_call x1, Pallas kernels, fast_device(): pl.pallas_call(functools.partial(pick_kernel, groups), in_specs=[in_smem,...  4.93 us

profile of v3, /device:TPU:8, one launch (start us, length us, event | category | flops | bytes accessed | tf_op | source)
XLA Modules:
  0.0 104.1 jit_solution(9532385188051900166)
XLA Ops:
  0.6 4.9 %pick_slots.1.packed_ref = bf16[8,304,256]{2,1,0:T(8,128)(2,1)} custom-call(s32[32]{0:T(128)} %bitcast.12, f32[273,8,224]{2,1,0:T(8,128)} %bitcast.8, f32[8,16,273]{2,1,0:T(8,128)} %bitcast.10, bf16[8,2,224]{2,1,0:T(2,128)(2,1)} %conv_ref.1), custom_call_target="tpu_custom_call" | custom-call | tf_op jit(solution)/shard_map/pick_slots/pallas_call | solution.py:807
  5.6 35.9 %gather_and_local_attention.1 = (f32[512,64]{1,0:T(8,128)}, bf16[512,256]{1,0:T(8,128)(2,1)}, f32[512,224]{1,0:T(8,128)}, f32[512,224]{1,0:T(8,128)}, f32[512,256]{1,0:T(8,128)}, /*index=5*/bf16[8,304,256]{2,1,0:T(8,128)(2,1)}) custom-call(s32[1,8]{1,0:T(1,128)} %lengths_ref.1, bf16[64,1792]{1,0:T(8,128)(2,1)} %own_ref.3, ...), custom_call_target="tpu_custom_call" | custom-call | tf_op jit(solution)/shard_map/gather_and_local_attention/pallas_call | solution.py:822
  41.5 11.1 %carried_states.1 = (bf16[512,256]{1,0:T(8,128)(2,1)}, bf16[512,224]{1,0:T(8,128)(2,1)}, f32[273,8,224]{2,1,0:T(8,128)}, bf16[16,384]{1,0:T(8,128)(2,1)}, bf16[8,2,224]{2,1,0:T(2,128)(2,1)}) custom-call(s32[32]{0:T(128)} %bitcast.13, s32[1,8]{1,0:T(1,128)} %lengths_ref.1, s32[8]{0:T(128)} %cached_ref.1, f32[512,64]{1,0:T(8,128)} %get-tuple-element.17.qk_ref, ...), custom_call_target="tpu_custom_call" | custom-call | tf_op jit(solution)/shard_map/carried_states/pallas_call | solution.py:852
  52.6 48.2 %sum_and_ffn.1 = (bf16[64,1792]{1,0:T(8,128)(2,1)}, bf16[8,16,384]{2,1,0:T(8,128)(2,1)}) custom-call(bf16[512,256]{1,0:T(8,128)(2,1)} %get-tuple-element.23.att_ref, bf16[512,224]{1,0:T(8,128)(2,1)} %get-tuple-element.24.gated_ref, bf16[2,224,1792]{2,1,0:T(8,128)(2,1)} %weight_ref.1, bf16[64,1792]{1,0:T(8,128)(2,1)} %own_ref.3, f32[2,1792]{1,0:T(2,128)} %gain_ref.3, ...), custom_call_target="tpu_custom_call" | custom-call | tf_op jit(solution)/shard_map/sum_and_ffn/pallas_call | solution.py:895
  100.8 0.9 slice_convert_fusion
  101.7 0.7 copy.25
  102.4 1.6 %copy.27 = bf16[64,1792]{1,0:T(8,128)(2,1)} copy(bf16[64,1792]{1,0:T(8,128)(2,1)} %get-tuple-element.34) | data formatting | bytes 458752
